TPU v7x, 512 devices: a whole 4x8x8 slice. The times are simulated.
512 devices in a mesh: slab: 16 (over z, core), fib: 32 (over x, y).
Axes of the slice: x: 4, y: 8, z: 8, core: 2. Of those that a mesh axis runs over, the one named last changes fastest.
Arguments:
- values: bfloat16 [16, 64, 64, 4096], P('slab', 'fib'), may hold values from -6 to 6
- observed: int32 [16, 64, 64, 4096], P('slab', 'fib'), may hold values 0 or 1
- coords: int32 [16, 64, 3], P('slab', 'fib'), may hold values from 0 to 31, as said below
- counts: int32 [16, 32], P('slab', 'fib'), may hold values from 1 to 2, as said below
- item_factors: float32 [4096, 32], P('fib'), may hold values from -6 to 6
- week_factors: float32 [2048, 32], P(('slab', 'fib')), may hold values from -0.06 to 0.06
Outputs:
- user_factors: float32 [4096, 32], P(('slab', 'fib'))
- item_updated: float32 [4096, 32], P('fib')
Inputs may be any that keep to these rules, and one draw needn't show every extreme that they name: `coords`: each row is a user block below 4, an item block below 2 and a week block below 32; the 2 rows of one device are distinct. `counts`: each device holds 1 or 2 live slots, its first ones; some device holds 2.
All inputs are finite; a program needn't handle non-finite values. No bound on the sum of `observed` on one device may be relied on, other than what follows from the above.
Results may differ from a plain program's by a relative error of at most 0.0029.
Values may be sent and summed in bfloat16 or wider, within the bound.
No kernel may reach another device: no remote copies, remote signals or barrier semaphores. Data moves between devices by JAX's collectives and lax.ppermute only.
A program may use at most 64 MiB of HBM per device.

v0:
```python
import jax
import jax.numpy as jnp
from jax import lax
from jax.sharding import PartitionSpec as P

B = 64
R = 32
UBD = 4
IBD = 2


ridge_weight = 1.0
precise = lax.Precision.HIGHEST
group_rows = 8


def pair_table(rows):
    return (rows[:, :, None] * rows[:, None, :]).reshape(rows.shape[0], -1)


def ridge_solve(gram, rhs):
    count, width = rhs.shape
    system = gram.reshape(count, width, width) + ridge_weight * jnp.eye(width, dtype=jnp.float32)
    factor = jnp.linalg.cholesky(system)
    return jax.scipy.linalg.cho_solve((factor, True), rhs[:, :, None])[:, :, 0]


def block_parts(values, observed, coords, slot, weeks_half):
    block_vals = lax.dynamic_index_in_dim(values[0], slot, 0, keepdims=False)
    block_mask = lax.dynamic_index_in_dim(observed[0], slot, 0, keepdims=False)
    place = lax.dynamic_index_in_dim(coords[0], slot, 0, keepdims=False)
    mask_half = block_mask.astype(jnp.bfloat16)
    weighted = (block_vals * mask_half).reshape(B, B, B)
    week_rows = lax.dynamic_slice_in_dim(weeks_half, place[2] * B, B, 0)
    moment = jnp.einsum("uiw,wr->uir", weighted, week_rows, preferred_element_type=jnp.float32)
    groups = mask_half.reshape(B // group_rows, group_rows, B, B)
    return (place, groups, moment)


def shards(values, observed, coords, counts, item_factors, week_factors):
    weeks_half = lax.all_gather(
        week_factors.astype(jnp.bfloat16), ("slab", "fib"), axis=0, tiled=True
    )
    week_pairs = pair_table(weeks_half.astype(jnp.float32)).astype(jnp.bfloat16)
    item_pairs = pair_table(item_factors)
    live_slots = counts[0, 0]
    width = R * R
    user_span = UBD * B
    item_span = IBD * B

    def user_block(slot, carry):
        gram, rhs = carry
        place, groups, moment = block_parts(values, observed, coords, slot, weeks_half)
        ubase = place[0] * B
        ibase = place[1] * B
        pair_rows = lax.dynamic_slice_in_dim(week_pairs, place[2] * B, B, 0)
        ipairs = lax.dynamic_slice_in_dim(item_pairs, ibase, B, 0)
        irows = lax.dynamic_slice_in_dim(item_factors, ibase, B, 0)

        def group_gram(group):
            cross = jnp.einsum("uiw,wk->uik", group, pair_rows, preferred_element_type=jnp.float32)
            return jnp.einsum("uik,ik->uk", cross, ipairs, precision=precise)

        gram_add = lax.map(group_gram, groups).reshape(B, width)
        rhs_add = jnp.einsum("uir,ir->ur", moment, irows, precision=precise)
        gram = lax.dynamic_update_slice_in_dim(
            gram, lax.dynamic_slice_in_dim(gram, ubase, B, 0) + gram_add, ubase, 0
        )
        rhs = lax.dynamic_update_slice_in_dim(
            rhs, lax.dynamic_slice_in_dim(rhs, ubase, B, 0) + rhs_add, ubase, 0
        )
        return (gram, rhs)

    start = (jnp.zeros((user_span, width), jnp.float32), jnp.zeros((user_span, R), jnp.float32))
    user_gram, user_rhs = lax.fori_loop(0, live_slots, user_block, start)
    own_users = user_span // lax.axis_size("fib")
    gram_all, rhs_all = lax.psum((user_gram, user_rhs), "fib")
    user_slab = ridge_solve(gram_all, rhs_all)
    user_out = lax.dynamic_slice_in_dim(user_slab, lax.axis_index("fib") * own_users, own_users, 0)
    user_pairs = pair_table(user_slab)

    def item_block(slot, carry):
        gram, rhs = carry
        place, groups, moment = block_parts(values, observed, coords, slot, weeks_half)
        ubase = place[0] * B
        ibase = place[1] * B
        pair_rows = lax.dynamic_slice_in_dim(week_pairs, place[2] * B, B, 0)
        upairs = lax.dynamic_slice_in_dim(user_pairs, ubase, B, 0)
        urows = lax.dynamic_slice_in_dim(user_slab, ubase, B, 0)

        def group_step(total, inputs):
            group, gpairs = inputs
            cross = jnp.einsum("uiw,wk->uik", group, pair_rows, preferred_element_type=jnp.float32)
            return (total + jnp.einsum("uik,uk->ik", cross, gpairs, precision=precise), None)

        gram_add, _ = lax.scan(
            group_step,
            jnp.zeros((B, width), jnp.float32),
            (groups, upairs.reshape(B // group_rows, group_rows, width)),
        )
        rhs_add = jnp.einsum("uir,ur->ir", moment, urows, precision=precise)
        gram = lax.dynamic_update_slice_in_dim(
            gram, lax.dynamic_slice_in_dim(gram, ibase, B, 0) + gram_add, ibase, 0
        )
        rhs = lax.dynamic_update_slice_in_dim(
            rhs, lax.dynamic_slice_in_dim(rhs, ibase, B, 0) + rhs_add, ibase, 0
        )
        return (gram, rhs)

    start = (jnp.zeros((item_span, width), jnp.float32), jnp.zeros((item_span, R), jnp.float32))
    item_gram, item_rhs = lax.fori_loop(0, live_slots, item_block, start)
    gram_all, rhs_all = lax.psum((item_gram, item_rhs), "slab")
    item_updated = ridge_solve(gram_all, rhs_all)
    return (user_out, item_updated)


def solution(mesh):
    in_specs = (
        P("slab", "fib", None, None),
        P("slab", "fib", None, None),
        P("slab", "fib", None),
        P("slab", "fib"),
        P("fib", None),
        P(("slab", "fib"), None),
    )
    out_specs = (P(("slab", "fib"), None), P("fib", None))
    return jax.shard_map(shards, mesh=mesh, in_specs=in_specs, out_specs=out_specs, check_vma=False)
```

profile of v0, /device:TPU:1, one launch (start us, length us, event | category | flops | bytes accessed | tf_op | source)
XLA Modules:
  0.0 1753.1 jit_solution(14195434211690385830)
XLA Ops:
  7.9 118.7 %all-gather = bf16[512,4,32]{2,1,0:T(4,128)(2,1)S(1)} all-gather(bf16[1,4,32]{2,1,0:T(4,128)(2,1)S(1)} %convert_bitcast_fusion), channel_id=1, replica_groups=mesh['slab'=16,'fib'=32] {'slab','fib'}, dimensions={0}, use_global_device_ids=true | all-gather | bytes 131328 | tf_op jit(solution)/shard_map/all_gather | solution.py:41
  126.8 3.0 multiply_convert_fusion
  129.9 6.6 copy.60
  139.3 28.3 %while.46 = (s32[]{:T(128)}, f32[256,1024]{1,0:T(8,128)}, f32[256,32]{1,0:T(8,128)}, s32[]{:T(128)}, s32[1,2,3]{2,1,0:T(2,128)}, /*index=5*/s32[1,2,64,4096]{3,2...) while((s32[]{:T(128)}, f32[256,1024]{1,0:T(8,128)}, ...), condition=%wide.region_3.4_spmd, body=%wide.region_0.3_spmd.sunk | while | flops 85778448 | bytes 8078378 | solution.py:75
  145.6 2.1 convert_element_type.54
  147.7 10.9 while.49
  159.2 1.7 fusion.52
  161.0 2.1 mul.141
  163.1 2.4 fusion.53
  171.0 139.9 %psum.29 = f32[256,32]{1,0:T(8,128)S(1)} all-reduce(f32[256,32]{1,0:T(8,128)S(1)} %copy-done.3), channel_id=1, replica_groups=mesh['slab'=16,'fib'=32] {'fib'}, use_global_device_ids=true, to_apply=%region_7.8 | all-reduce | flops 8192 | bytes 65536 | tf_op jit(solution)/shard_map/psum | solution.py:77
  311.0 39.0 %all-reduce.3.cloned.1.call-done = f32[256,32,32]{0,1,2:T(8,128)} async-done(((f32[256,32,32]{0,1,2:T(8,128)}), f32[256,32,32]{0,1,2:T(8,128)}) %all-reduce.3.cloned.1.call-update) | async-done | bytes 1048592 | tf_op jit(solution)/shard_map/psum | solution.py:77
  352.0 4.4 copy.67
  356.4 4.7 broadcast_multiply_fusion
  361.0 751.5 %custom-call.22 = f32[256,32,32]{2,1,0:T(8,128)} custom-call(f32[256,32,32]{2,1,0:T(8,128)} %broadcast_multiply_fusion), custom_call_target="Cholesky" | custom-call | tf_op jit(solution)/shard_map/jit(cholesky)/cholesky | solution.py:24
  1112.6 3.5 copy.68
  1117.5 25.8 %custom-call.23 = f32[256,1,32,32]{0,2,3,1:T(8,128)S(1)} custom-call(f32[256,1,32,32]{0,3,2,1:T(8,128)} %select_bitcast_fusion), custom_call_target="InvertDiagBlocksLowerTriangular" | custom-call | tf_op jit(solution)/shard_map/jit(_cho_solve)/vmap()/triangular_solve | solution.py:25
  1143.4 4.4 copy.111
  1147.8 5.9 convolution_bitcast_fusion.2
  1153.7 6.6 fusion.24
  1163.9 29.8 %while.48 = (s32[]{:T(128)}, f32[128,1024]{1,0:T(8,128)}, f32[128,32]{1,0:T(8,128)}, s32[]{:T(128)}, s32[1,2,3]{2,1,0:T(2,128)}, /*index=5*/s32[1,2,64,4096]{3,2...) while((s32[]{:T(128)}, f32[128,1024]{1,0:T(8,128)}, ...), condition=%wide.region_11.12_spmd, body=%wide.region_8.11_spmd.sunk | while | flops 85852176 | bytes 8881228 | solution.py:111
  1170.2 2.1 convert_element_type.55
  1172.3 11.8 while.50
  1187.1 2.1 mul.146
  1189.2 2.4 fusion.58
  1196.1 78.2 %psum.31 = f32[128,32]{1,0:T(8,128)S(1)} all-reduce(f32[128,32]{1,0:T(8,128)} %get-tuple-element.177), channel_id=1, replica_groups=mesh['slab'=16,'fib'=32] {'slab'}, use_global_device_ids=true, to_apply=%region_15.16 | all-reduce | flops 4096 | bytes 32768 | tf_op jit(solution)/shard_map/psum | solution.py:112
  1275.6 67.7 %all-reduce.5.cloned.1.call-done = f32[128,32,32]{0,1,2:T(8,128)} async-done(((f32[128,32,32]{0,1,2:T(8,128)}), f32[128,32,32]{0,1,2:T(8,128)}) %all-reduce.5.cloned.1.call-update) | async-done | bytes 524304 | tf_op jit(solution)/shard_map/psum | solution.py:112
  1344.8 1.8 copy.79
  1348.3 376.4 %custom-call.24 = f32[128,32,32]{2,1,0:T(8,128)} custom-call(f32[128,32,32]{2,1,0:T(8,128)} %broadcast_multiply_fusion.1), custom_call_target="Cholesky" | custom-call | tf_op jit(solution)/shard_map/jit(cholesky)/cholesky | solution.py:24
  1724.7 2.7 copy.80
  1727.8 12.5 custom-call.25
  1740.3 1.9 copy.114
  1742.2 3.4 fusion.25
  (116 shorter events, 58.3 us)
Async XLA Ops:
  7.2 342.8 %all-reduce.3.cloned.1.call-start = ((), (), s32[]{:S(2)}) async-start(), calls=%async_computation | async-start | bytes 2097152 | tf_op jit(solution)/shard_map/psum | solution.py:77
  126.8 3.1 copy-start.5
  129.9 6.6 copy-start.4
  129.9 9.4 copy-start
  167.6 3.4 copy-start.3
  170.9 1172.4 %all-reduce.5.cloned.1.call-start = ((), (), s32[]{:S(2)}) async-start(), calls=%async_computation.1 | async-start | bytes 1048576 | tf_op jit(solution)/shard_map/psum | solution.py:112
  310.9 805.2 %copy-start.8 = (pred[32,32]{1,0:T(8,128)(4,1)}, pred[32,32]{1,0:T(8,128)(4,1)S(1)}, u32[]{:S(2)}) copy-start(pred[32,32]{1,0:T(8,128)(4,1)S(1)} %iota_compare_fusion) | copy-start | bytes 3076
  311.0 805.4 %copy-start.6 = (pred[32,32]{1,0:T(8,128)(4,1)}, pred[32,32]{1,0:T(8,128)(4,1)S(1)}, u32[]{:S(2)}) copy-start(pred[32,32]{1,0:T(8,128)(4,1)S(1)} %iota_compare_fusion.1) | copy-start | bytes 3076
  1147.8 5.9 copy-start.1
  1160.3 0.7 copy-start.2
  1344.8 382.5 %copy-start.9 = (pred[32,32]{1,0:T(8,128)(4,1)S(1)}, pred[32,32]{1,0:T(8,128)(4,1)}, u32[]{:S(2)}) copy-start(pred[32,32]{1,0:T(8,128)(4,1)} %copy-done.8) | copy-start | bytes 3076
  1346.7 380.9 %copy-start.7 = (pred[32,32]{1,0:T(8,128)(4,1)S(1)}, pred[32,32]{1,0:T(8,128)(4,1)}, u32[]{:S(2)}) copy-start(pred[32,32]{1,0:T(8,128)(4,1)} %copy-done.6) | copy-start | bytes 3076
Sparse Core Ops, SparseCore 0:
  171.0 178.9 all-reduce.2
  1196.2 147.0 all-reduce.4
where the time goes:
time: 1760 us; the launch traced here: 1750 us
  other arithmetic  1190 us (68%)
  blocking collectives  337 us (19%)
  waiting for transfers between devices  107 us (6%)
  local copies, waits for them, and re-layouts  54.7 us (3%)
  matrix products  41.9 us (2%)
    another operation x7, other arithmetic, ridge_solve(): factor = jnp.linalg.cholesky(system)  1130 us
    psum x1, blocking collectives, shards(): gram_all, rhs_all = lax.psum((user_gram, user_rhs), 'fib')  140 us
    all_gather x1, blocking collectives, shards(): lax.all_gather(week_factors.astype(jnp.bfloat16), ('slab', 'fib'), axis=0...  119 us
    psum x1, blocking collectives, shards(): gram_all, rhs_all = lax.psum((item_gram, item_rhs), 'slab')  78.2 us
    psum x1, waiting for transfers between devices, shards(): gram_all, rhs_all = lax.psum((item_gram, item_rhs), 'slab')  67.7 us
    another operation x6, other arithmetic, ridge_solve(): return jax.scipy.linalg.cho_solve((factor, True), rhs[:, :, None])[:, :, 0]  40.4 us
    psum x1, waiting for transfers between devices, shards(): gram_all, rhs_all = lax.psum((user_gram, user_rhs), 'fib')  39 us
  transfers between devices with their start and end apart: 2, of which 2 were waited for; matrix products, arithmetic and copies ran while one was open for 0% of the time, Pallas kernels for 0%

commit v1 on v0

v1 whole, which is shorter than its diff:
```python
import jax
import jax.numpy as jnp
import numpy as np
from jax import lax
from jax.experimental import pallas as pl
from jax.experimental.pallas import tpu as pltpu
from jax.sharding import PartitionSpec as P

B = 64
R = 32
UBD = 4
IBD = 2
T = 8
LANES = 128
SIDE = 4
CHUNK = SIDE * B
PACK = LANES // R
WROWS = B // PACK
ridge_weight = 1.0
precise = lax.Precision.HIGHEST
LINK = jnp.bfloat16
f32 = jnp.float32
bf16 = jnp.bfloat16


def tables():
    start, left, right = {}, [], []
    for r in range(R):
        start[r] = len(left)
        for s in range(r // T * T, R):
            left.append(r)
            right.append(s)
    width = len(left)
    one = np.zeros((R, width), np.float32)
    two = np.zeros((R, width), np.float32)
    for k, (r, s) in enumerate(zip(left, right)):
        if s >= r:
            one[r, k] = 1
            two[s, k] = 1
    put = np.zeros((LANES, width), np.float32)
    for j in range(R // T):
        row5, row6, row7 = (start[j * T + n] for n in (5, 6, 7))
        for n in range(7):
            put[j * T + n, row7 + n] = 1
        put[j * T + 7, row6] = 1
        for n in range(1, 6):
            put[R + j * T + n, row6 + n] = 1
        put[R + j * T, row5] = 1
        put[R + j * T + 6, row5 + 1] = 1
        put[R + j * T + 7, row5 + 2] = 1
    return start, width, one, two, put


START, WIDTH, ONE, TWO, PUT = tables()


def dot(a, b, dims=(1, 0), precision=None):
    return lax.dot_general(
        a, b, (((dims[0],), (dims[1],)), ((), ())), preferred_element_type=f32, precision=precision
    )


def iota(shape, dim):
    return lax.broadcasted_iota(jnp.int32, shape, dim)


def week_block(weeks, wide_one, wide_two, start):
    packed = weeks[pl.ds(pl.multiple_of(start * WROWS, WROWS), WROWS), :]
    spread = (iota((B, WROWS), 0) // PACK == iota((B, WROWS), 1)).astype(f32).astype(bf16)
    rows = dot(spread, packed)
    own = iota((B, LANES), 0) % PACK == iota((B, LANES), 1) // R
    rows = jnp.where(own, rows, 0.0).astype(bf16)
    pairs = (dot(rows, wide_one[...]) * dot(rows, wide_two[...])).astype(bf16).astype(f32)
    fold = (iota((LANES, LANES), 0) % R == iota((LANES, LANES), 1) % R).astype(f32).astype(bf16)
    return pairs, dot(rows, fold)


def split(x):
    high = x.astype(bf16).astype(f32)
    return jnp.where(iota(x.shape, 1) < R, high, x - high).astype(bf16)


def repeat_rows(rows):
    return jnp.concatenate([rows] * PACK, axis=1)


def join(x):
    return x[:, :R] + x[:, R:2 * R]


def send_form(gram, rhs, put):
    parts = split(repeat_rows(rhs))
    parts = jnp.where(iota(parts.shape, 1) < 2 * R, parts.astype(f32), 0.0).astype(bf16)
    return (gram + dot(parts, put[...])).astype(LINK)


def block_arrays(values, observed, slot):
    mask = observed[slot].astype(f32)
    return mask.astype(bf16), (values[slot].astype(f32) * mask).astype(bf16)


def user_kernel(coords, counts, values, observed, items, weeks, one, two, wide_one, wide_two, put, out, gram, rhs):
    gram[...] = jnp.zeros_like(gram)
    rhs[...] = jnp.zeros_like(rhs)

    def block(slot):
        ubase = pl.multiple_of(coords[slot, 0] * B, B)
        ibase = pl.multiple_of(coords[slot, 1] * B, B)
        wpairs, wrows = week_block(weeks, wide_one, wide_two, coords[slot, 2])
        rows = items[pl.ds(ibase, B), :]
        ipairs = dot(rows, one[...], precision=precise) * dot(rows, two[...], precision=precise)
        irows = repeat_rows(rows)
        mask, weighted = block_arrays(values, observed, slot)
        gram_add = jnp.zeros((B, WIDTH), f32)
        rhs_add = jnp.zeros((B, LANES), f32)
        for c in range(B // SIDE):
            here = slice(c * SIDE, (c + 1) * SIDE)
            cells = slice(c * CHUNK, (c + 1) * CHUNK)
            outer = (ipairs[here][:, None, :] * wpairs[None]).reshape(CHUNK, WIDTH).astype(bf16)
            gram_add += dot(mask[:, cells], outer)
            outer = split((irows[here][:, None, :] * wrows[None]).reshape(CHUNK, LANES))
            rhs_add += dot(weighted[:, cells], outer)
        gram[pl.ds(ubase, B), :] += gram_add
        rhs[pl.ds(ubase, B), :] += join(rhs_add)

    block(0)

    @pl.when(counts[0, 0] > 1)
    def _():
        block(1)

    out[...] = send_form(gram[...], rhs[...], put)


def item_kernel(coords, counts, values, observed, users, weeks, one, two, wide_one, wide_two, put, out, gram, rhs):
    gram[...] = jnp.zeros_like(gram)
    rhs[...] = jnp.zeros_like(rhs)

    def block(slot):
        ubase = pl.multiple_of(coords[slot, 0] * B, B)
        ibase = pl.multiple_of(coords[slot, 1] * B, B)
        wpairs, wrows = week_block(weeks, wide_one, wide_two, coords[slot, 2])
        rows = users[pl.ds(ubase, B), :]
        upairs = dot(rows, one[...], precision=precise) * dot(rows, two[...], precision=precise)
        upairs = upairs.astype(bf16)
        urows = split(repeat_rows(rows))
        mask, weighted = block_arrays(values, observed, slot)
        gram_add, rhs_add = [], []
        for c in range(B // SIDE):
            cells = slice(c * CHUNK, (c + 1) * CHUNK)
            cross = dot(mask[:, cells], upairs, (0, 0)).reshape(SIDE, B, WIDTH)
            gram_add.append(jnp.sum(cross * wpairs[None], axis=1))
            moment = dot(weighted[:, cells], urows, (0, 0)).reshape(SIDE, B, LANES)
            rhs_add.append(jnp.sum(moment * wrows[None], axis=1))
        gram[pl.ds(ibase, B), :] += jnp.concatenate(gram_add, axis=0)
        rhs[pl.ds(ibase, B), :] += join(jnp.concatenate(rhs_add, axis=0))

    block(0)

    @pl.when(counts[0, 0] > 1)
    def _():
        block(1)

    out[...] = send_form(gram[...], rhs[...], put)


def solve_kernel(parts, out, copies):
    count = parts.shape[0]
    pick = (iota((count, LANES), 0) % T == iota((count, LANES), 1)).astype(f32)
    if LINK == bf16:
        packed = dot(parts[...], pick.astype(bf16), (0, 0))
    else:
        packed = dot(parts[...], pick, (0, 0), precise)
    sub = iota((T, LANES), 0)

    def tile(r, t):
        first = START[r] + (t - r // T) * T
        return packed[first:first + T]

    def spread(x, n):
        return jnp.broadcast_to(x[n:n + 1], (T, LANES))

    tiles = R // T
    rows = {}
    for r in range(R):
        for t in range(r // T, tiles):
            x = tile(r, t)
            rows[r, t] = x + jnp.where(sub == r % T, ridge_weight, 0.0) if t == r // T else x
    side = []
    for j in range(tiles):
        row5, row6, row7 = (tile(j * T + n, j) for n in (5, 6, 7))
        high = jnp.where(sub == 7, spread(row6, 0), row7)
        low = jnp.where(sub == 0, row5, row6)
        low = jnp.where(sub == 6, spread(row5, 1), low)
        low = jnp.where(sub == 7, spread(row5, 2), low)
        side.append(high + low)
    factor, right = {}, []
    for k in range(R):
        own = k // T
        inverse = 1.0 / spread(rows[k, own], k % T)
        scaled = {t: rows[k, t] * inverse for t in range(own, tiles)}
        mine = spread(side[own], k % T)
        right.append(mine * inverse)
        for t in range(own, tiles):
            side[t] = side[t] - scaled[t] * mine
        for r in range(k + 1, R):
            factor[k, r] = spread(scaled[r // T], r % T)
            for t in range(r // T, tiles):
                rows[r, t] = rows[r, t] - factor[k, r] * rows[k, t]
    answer = []
    for s in range(R - 1, -1, -1):
        for k in range(s):
            right[k] = right[k] - factor[k, s] * right[s]
    for j in range(tiles):
        x = right[j * T]
        for n in range(1, T):
            x = jnp.where(sub == n, right[j * T + n], x)
        answer.append(x)
    answer = jnp.concatenate(answer, axis=0)
    answer = jnp.transpose(answer)[:T, :]
    out[...] = answer
    copies[...] = jnp.broadcast_to(answer[None], copies.shape)


def vmem():
    return pl.BlockSpec(memory_space=pltpu.VMEM)


def smem():
    return pl.BlockSpec(memory_space=pltpu.SMEM)


PARAMS = pltpu.CompilerParams(vmem_limit_bytes=48 * 1024 * 1024)


def normal_equations(kernel, span, coords, counts, values, observed, factors, weeks, consts):
    return pl.pallas_call(
        kernel,
        out_shape=jax.ShapeDtypeStruct((span, WIDTH), LINK),
        in_specs=[smem(), smem()] + [vmem()] * (4 + len(consts)),
        out_specs=vmem(),
        scratch_shapes=[pltpu.VMEM((span, WIDTH), f32), pltpu.VMEM((span, R), f32)],
        compiler_params=PARAMS,
    )(coords, counts, values, observed, factors, weeks, *consts)


def solve(parts, peers):
    return pl.pallas_call(
        solve_kernel,
        out_shape=(jax.ShapeDtypeStruct((T, R), f32), jax.ShapeDtypeStruct((peers, T, R), f32)),
        in_specs=[vmem()],
        out_specs=(vmem(), vmem()),
        compiler_params=PARAMS,
    )(parts)


def to_all(x, axis):
    copies = jnp.broadcast_to(x[None], (lax.axis_size(axis),) + x.shape)
    return lax.all_to_all(copies, axis, 0, 0, tiled=True)


def shards(values, observed, coords, counts, item_factors, week_factors):
    n_slab, n_fib = lax.axis_size("slab"), lax.axis_size("fib")
    consts = (
        jnp.asarray(ONE), jnp.asarray(TWO),
        jnp.asarray(np.tile(ONE, (PACK, 1)), bf16), jnp.asarray(np.tile(TWO, (PACK, 1)), bf16),
        jnp.asarray(PUT, bf16),
    )
    packed = week_factors.astype(bf16).reshape(1, LANES)
    weeks = to_all(packed, "fib").reshape(n_fib, LANES)
    weeks = to_all(weeks, "slab").reshape(n_slab * n_fib, LANES)
    shared = (coords[0], counts, values[0], observed[0])
    parts = normal_equations(user_kernel, UBD * B, *shared, item_factors, weeks, consts)
    parts = lax.all_to_all(parts, "fib", 0, 0, tiled=True)
    user_out, copies = solve(parts, n_fib)
    users = lax.all_to_all(copies, "fib", 0, 0, tiled=True).reshape(UBD * B, R)
    parts = normal_equations(item_kernel, IBD * B, *shared, users, weeks, consts)
    parts = lax.all_to_all(parts, "slab", 0, 0, tiled=True)
    _, copies = solve(parts, n_slab)
    item_updated = lax.all_to_all(copies, "slab", 0, 0, tiled=True).reshape(IBD * B, R)
    return (user_out, item_updated)


def solution(mesh):
    in_specs = (
        P("slab", "fib", None, None),
        P("slab", "fib", None, None),
        P("slab", "fib", None),
        P("slab", "fib"),
        P("fib", None),
        P(("slab", "fib"), None),
    )
    out_specs = (P(("slab", "fib"), None), P("fib", None))
    return jax.shard_map(shards, mesh=mesh, in_specs=in_specs, out_specs=out_specs, check_vma=False)
```

time: 1760 us -> 132 us (0.07)
  other arithmetic: 1190 us -> 3.5 us
  blocking collectives: 337 us -> 77.3 us
  waiting for transfers between devices: 107 us -> 7.08 us
  matrix products: 41.9 us -> 0 us
  local copies, waits for them, and re-layouts: 54.7 us -> 19.9 us
    another operation x14 -> x0, other arithmetic: 1170 us -> none  [the longest x7 1130 us: ridge_solve(): factor = jnp.linalg.cholesky(system)]
    psum x2 -> x0, blocking collectives: 218 us -> none  [the longest x1 140 us: shards(): gram_all, rhs_all = lax.psum((user_gram, user_rhs), 'fib')]
    all_gather x1 -> x0, blocking collectives: 119 us -> none  [shards(): lax.all_gather(week_factors.astype(jnp.bfloat16), ('slab', 'fib'), axis=0...]
    psum x2 -> x0, waiting for transfers between devices: 107 us -> none  [the longest x1 67.7 us: shards(): gram_all, rhs_all = lax.psum((item_gram, item_rhs), 'slab')]
    all_to_all x0 -> x5, blocking collectives: none -> 77.3 us  [the longest x1 18.9 us: to_all(): return lax.all_to_all(copies, axis, 0, 0, tiled=True)]
    dot_general x18 -> x0, matrix products: 26.1 us -> none  [the longest x8 10.7 us: group_step(): jnp.einsum('uiw,wk->uik', group, pair_rows, preferred_element_type=jnp.fl...]
    unnamed x21 -> x45, local copies, waits for them, and re-layouts: 0.75 us -> 18.6 us
  transfers between devices with their start and end apart: 2 -> 1, of which waited for: 2 -> 1; matrix products, arithmetic and copies ran while one was open for 0% -> 1% of each run, Pallas kernels for 0% -> 0%
where the time goes in v1:
time: 132 us; the launch traced here: 131 us
  blocking collectives  77.3 us (59%)
  local copies, waits for them, and re-layouts  19.9 us (15%)
  starting transfers between devices  12.4 us (9%)
  Pallas kernels  9.11 us (7%)
  waiting for transfers between devices  7.08 us (5%)
  other arithmetic  3.5 us (3%)
  between operations  1.38 us (1%)
    all_to_all x1, blocking collectives, to_all(): return lax.all_to_all(copies, axis, 0, 0, tiled=True)  18.9 us
    unnamed x45, local copies, waits for them, and re-layouts  18.6 us
    all_to_all x1, blocking collectives, shards(): parts = lax.all_to_all(parts, 'slab', 0, 0, tiled=True)  16.9 us
    all_to_all x1, blocking collectives, shards(): parts = lax.all_to_all(parts, 'fib', 0, 0, tiled=True)  16.2 us
    all_to_all x1, blocking collectives, shards(): users = lax.all_to_all(copies, 'fib', 0, 0, tiled=True).reshape(UBD * B, R)  15.6 us
    all_to_all x1, starting transfers between devices, to_all(): return lax.all_to_all(copies, axis, 0, 0, tiled=True)  12.4 us
    all_to_all x1, blocking collectives, shards(): lax.all_to_all(copies, 'slab', 0, 0, tiled=True).reshape(IBD * B, R)  9.78 us
    all_to_all x1, waiting for transfers between devices, to_all(): return lax.all_to_all(copies, axis, 0, 0, tiled=True)  7.08 us
  transfers between devices with their start and end apart: 1, of which 1 were waited for; matrix products, arithmetic and copies ran while one was open for 1% of the time, Pallas kernels for 0%

profile of v1, /device:TPU:1, one launch (start us, length us, event | category | flops | bytes accessed | tf_op | source)
XLA Modules:
  0.0 130.7 jit_solution(17465043150830657156)
XLA Ops:
  0.6 0.7 convert_element_type.3
  1.4 18.9 %all_to_all.42 = bf16[32,1,128]{2,1,0:T(2,128)(2,1)S(1)} all-to-all(bf16[32,1,128]{2,1,0:T(2,128)(2,1)S(1)} %broadcast_in_dim.15), channel_id=1, replica_groups=mesh['slab'=16,'fib'=32] {'fib'}, dimensions={0} | all-to-all | bytes 16384 | tf_op jit(solution)/shard_map/all_to_all | solution.py:259
  20.4 0.7 broadcast_in_dim.17
  21.0 12.4 %all-to-all-start.1 = ((bf16[16,32,128]{2,1,0:T(8,128)(2,1)}), bf16[16,32,128]{2,1,0:T(8,128)(2,1)S(1)}, u32[]{:S(2)}, u32[]{:S(2)}) async-start(bf16[16,32,128]{2,1,0:T(8,128)(2,1)} %broadcast_in_dim.17), calls=%async_computation.1 | async-start | bytes 262144 | tf_op jit(solution)/shard_map/all_to_all | solution.py:259
  34.1 1.4 %copy.17.items = f32[128,32]{1,0:T(8,128)} copy(f32[128,32]{0,1:T(8,128)} %param.15) | data formatting | bytes 32768 | tf_op args[4]
  35.6 7.1 %all-to-all-done.1 = bf16[16,32,128]{2,1,0:T(8,128)(2,1)S(1)} async-done(((bf16[16,32,128]{2,1,0:T(8,128)(2,1)}), bf16[16,32,128]{2,1,0:T(8,128)(2,1)S(1)}, u32[]{:S(2)}, u32[]{:S(2)}) %all-to-all-start.1) | async-done | bytes 131104 | tf_op jit(solution)/shard_map/all_to_all | solution.py:259
  42.6 1.6 %copy-done = s32[1,2,64,4096]{3,2,1,0:T(8,128)S(1)} copy-done((s32[1,2,64,4096]{3,2,1,0:T(8,128)S(1)}, s32[1,2,64,4096]{3,2,1,0:T(8,128)}, u32[]{:S(2)}) %copy-start) | copy-done | bytes 2097176
  44.2 1.2 copy-done.2
  45.5 0.9 copy-done.4
  46.4 0.9 copy-done.6
  47.3 0.9 copy-done.8
  48.2 0.9 copy-done.11
  49.1 0.9 copy-done.13
  50.0 0.8 copy-done.15
  50.8 0.7 copy-done.17
  51.5 3.0 %shard_map.122 = bf16[256,640]{1,0:T(8,128)(2,1)S(1)} custom-call(s32[2,3]{1,0:T(2,128)S(1)} %bitcast.24, s32[1,1]{1,0:T(1,128)S(6)} %copy.22.counts, bf16[2,64,4096]{2,1,0:T(8,128)(2,1)S(1)} %bitcast.15, s32[2,64,4096]{2,1,0:T(8,128)S(1)} %bitcast.13, f32[128,32]{1,0:T(8,128)S(1)} %copy-done.15, bf16[512,128]{1,0:T(8,128)(2,1)S(1)} %bitcast.19, ...), custom_call_target="tpu_custom_call" | custom-call | tf_op jit(solution)/shard_map/pallas_call | solution.py:237
  54.5 16.2 %all_to_all.43 = bf16[32,8,640]{2,1,0:T(8,128)(2,1)S(1)} all-to-all(bf16[32,8,640]{2,1,0:T(8,128)(2,1)S(1)} %bitcast.17), channel_id=1, replica_groups=mesh['slab'=16,'fib'=32] {'fib'}, dimensions={0} | all-to-all | bytes 655360 | tf_op jit(solution)/shard_map/all_to_all | solution.py:274
  70.7 1.4 %shard_map.123 = (f32[8,32]{1,0:T(8,128)}, f32[32,8,32]{2,1,0:T(8,128)S(1)}) custom-call(bf16[256,640]{1,0:T(8,128)(2,1)S(1)} %bitcast.18), custom_call_target="tpu_custom_call" | custom-call | tf_op jit(solution)/shard_map/pallas_call | solution.py:248
  72.8 1.6 %reshape.24 = f32[32,1,256]{2,1,0:T(1,128)} reshape(f32[32,8,32]{2,1,0:T(8,128)} %copy-done.16) | data formatting | bytes 65536
  74.4 15.6 %all_to_all.44 = f32[32,1,256]{2,1,0:T(1,128)} all-to-all(f32[32,1,256]{2,1,0:T(1,128)} %reshape.24), channel_id=1, replica_groups=mesh['slab'=16,'fib'=32] {'fib'}, dimensions={0} | all-to-all | bytes 65536 | tf_op jit(solution)/shard_map/all_to_all | solution.py:276
  90.5 2.1 %reduce = f32[32,256]{1,0:T(8,128)} reduce(f32[32,1,256]{2,1,0:T(1,128)} %all_to_all.44, f32[]{:T(128)} %broadcast.1), dimensions={1}, to_apply=%all_to_all.31.reduce_sub_computation | reduce | bytes 65540 | tf_op jit(solution)/shard_map/all_to_all | solution.py:276
  92.6 1.5 %reshape.25 = f32[32,8,32]{2,1,0:T(8,128)} reshape(f32[32,256]{1,0:T(8,128)} %reduce) | data formatting | bytes 65536
  94.2 0.9 copy-done.7
  95.1 0.9 copy-done.9
  96.0 0.9 copy-done.10
  96.9 0.9 copy-done.14
  97.8 3.3 %shard_map.124 = bf16[128,640]{1,0:T(8,128)(2,1)S(1)} custom-call(s32[2,3]{1,0:T(2,128)S(1)} %bitcast.25, s32[1,1]{1,0:T(1,128)S(6)} %copy.22.counts, bf16[2,64,4096]{2,1,0:T(8,128)(2,1)S(1)} %bitcast.16, s32[2,64,4096]{2,1,0:T(8,128)S(1)} %bitcast.14, f32[256,32]{1,0:T(8,128)S(1)} %bitcast.23, bf16[512,128]{1,0:T(8,128)(2,1)S(1)} %bitcast.20, ...), custom_call_target="tpu_custom_call" | custom-call | tf_op jit(solution)/shard_map/pallas_call | solution.py:237
  101.1 16.9 %all_to_all.45 = bf16[16,8,640]{2,1,0:T(8,128)(2,1)S(1)} all-to-all(bf16[16,8,640]{2,1,0:T(8,128)(2,1)S(1)} %bitcast.21), channel_id=1, replica_groups=mesh['slab'=16,'fib'=32] {'slab'}, dimensions={0} | all-to-all | bytes 327680 | tf_op jit(solution)/shard_map/all_to_all | solution.py:278
  118.0 1.4 %shard_map.125 = (f32[8,32]{1,0:T(8,128)}, f32[16,8,32]{2,1,0:T(8,128)S(1)}) custom-call(bf16[128,640]{1,0:T(8,128)(2,1)S(1)} %bitcast.22), custom_call_target="tpu_custom_call" | custom-call | tf_op jit(solution)/shard_map/pallas_call | solution.py:248
  119.5 9.8 %all_to_all.46 = f32[16,1,256]{2,1,0:T(1,128)S(1)} all-to-all(f32[16,1,256]{2,1,0:T(1,128)S(1)} %reshape.26), channel_id=1, replica_groups=mesh['slab'=16,'fib'=32] {'slab'}, dimensions={0} | all-to-all | bytes 32768 | tf_op jit(solution)/shard_map/all_to_all | solution.py:280
  129.3 0.7 reduce.1
  130.1 0.7 copy.18
  (31 shorter events, 1.5 us)
Async XLA Ops:
  21.0 21.6 %all-to-all-start.1 = ((bf16[16,32,128]{2,1,0:T(8,128)(2,1)}), bf16[16,32,128]{2,1,0:T(8,128)(2,1)S(1)}, u32[]{:S(2)}, u32[]{:S(2)}) async-start(bf16[16,32,128]{2,1,0:T(8,128)(2,1)} %broadcast_in_dim.17), calls=%async_computation.1 | async-start | bytes 262144 | tf_op jit(solution)/shard_map/all_to_all | solution.py:259
  42.6 1.6 %copy-start = (s32[1,2,64,4096]{3,2,1,0:T(8,128)S(1)}, s32[1,2,64,4096]{3,2,1,0:T(8,128)}, u32[]{:S(2)}) copy-start(s32[1,2,64,4096]{3,2,1,0:T(8,128)} %param.12) | copy-start | bytes 6291460
  44.2 1.2 copy-start.2
  45.5 0.9 copy-start.4
  46.4 0.9 copy-start.6
  47.3 0.9 copy-start.8
  48.2 0.9 copy-start.11
  49.1 0.9 copy-start.13
  50.0 0.8 copy-start.15
  50.8 0.7 copy-start.17
  51.5 42.6 %copy-start.1 = (s32[1,2,64,4096]{3,2,1,0:T(8,128)S(1)}, s32[1,2,64,4096]{3,2,1,0:T(8,128)}, u32[]{:S(2)}) copy-start(s32[1,2,64,4096]{3,2,1,0:T(8,128)} %param.12) | copy-start | bytes 6291460
  51.5 42.6 %copy-start.3 = (bf16[1,2,64,4096]{3,2,1,0:T(8,128)(2,1)S(1)}, bf16[1,2,64,4096]{3,2,1,0:T(8,128)(2,1)}, u32[]{:S(2)}) copy-start(bf16[1,2,64,4096]{3,2,1,0:T(8,128)(2,1)} %param.11) | copy-start | bytes 3145732
  51.5 42.6 %copy-start.5 = (bf16[128,640]{1,0:T(8,128)(2,1)S(1)}, bf16[128,640]{1,0:T(8,128)(2,1)}, u32[]{:S(2)}) copy-start(bf16[128,640]{1,0:T(8,128)(2,1)} %constant.12.clone.wide_one) | copy-start | bytes 491524
  51.5 42.6 %copy-start.12 = (f32[32,640]{1,0:T(8,128)S(1)}, f32[32,640]{1,0:T(8,128)}, u32[]{:S(2)}) copy-start(f32[32,640]{1,0:T(8,128)} %constant.10.clone.one) | copy-start | bytes 245764
  51.5 42.6 %copy-start.18 = (s32[1,2,3]{2,1,0:T(2,128)S(1)}, s32[1,2,3]{2,1,0:T(2,128)}, u32[]{:S(2)}) copy-start(s32[1,2,3]{2,1,0:T(2,128)} %param.13) | copy-start | bytes 76
  72.1 0.7 copy-start.16
  94.2 0.9 copy-start.7
  95.1 0.9 copy-start.9
  96.0 0.9 copy-start.10
  96.9 0.9 copy-start.14

commit v2 on v1

v2 whole, which is shorter than its diff:
```python
import jax
import jax.numpy as jnp
import numpy as np
from jax import lax
from jax.experimental import pallas as pl
from jax.experimental.pallas import tpu as pltpu
from jax.sharding import PartitionSpec as P

B = 64
R = 32
UBD = 4
IBD = 2
T = 8
LANES = 128
SIDE = 4
CHUNK = SIDE * B
PACK = LANES // R
WROWS = B // PACK
ridge_weight = 1.0
precise = lax.Precision.HIGHEST
LINK = jnp.bfloat16
f32 = jnp.float32
bf16 = jnp.bfloat16


def tables():
    start, left, right = {}, [], []
    for r in range(R):
        start[r] = len(left)
        for s in range(r // T * T, R):
            left.append(r)
            right.append(s)
    width = len(left)
    one = np.zeros((R, width), np.float32)
    two = np.zeros((R, width), np.float32)
    for k, (r, s) in enumerate(zip(left, right)):
        if s >= r:
            one[r, k] = 1
            two[s, k] = 1
    put = np.zeros((LANES, width), np.float32)
    for j in range(R // T):
        row5, row6, row7 = (start[j * T + n] for n in (5, 6, 7))
        for n in range(7):
            put[j * T + n, row7 + n] = 1
        put[j * T + 7, row6] = 1
        for n in range(1, 6):
            put[R + j * T + n, row6 + n] = 1
        put[R + j * T, row5] = 1
        put[R + j * T + 6, row5 + 1] = 1
        put[R + j * T + 7, row5 + 2] = 1
    return start, width, one, two, put


START, WIDTH, ONE, TWO, PUT = tables()
TABLE = np.concatenate([ONE, TWO, PUT[:2 * R]])


def dot(a, b, dims=(1, 0), precision=None):
    return lax.dot_general(
        a, b, (((dims[0],), (dims[1],)), ((), ())), preferred_element_type=f32, precision=precision
    )


def iota(shape, dim):
    return lax.broadcasted_iota(jnp.int32, shape, dim)


def week_block(weeks, one, two, start):
    packed = weeks[pl.ds(pl.multiple_of(start * WROWS, WROWS), WROWS), :]
    spread = (iota((B, WROWS), 0) // PACK == iota((B, WROWS), 1)).astype(f32).astype(bf16)
    rows = dot(spread, packed)
    own = iota((B, LANES), 0) % PACK == iota((B, LANES), 1) // R
    rows = jnp.where(own, rows, 0.0).astype(bf16)
    pairs = dot(rows, jnp.concatenate([one] * PACK)) * dot(rows, jnp.concatenate([two] * PACK))
    return pairs.astype(bf16), dot(rows, fold()).astype(bf16)


def fold():
    return (iota((LANES, LANES), 0) % R == iota((LANES, LANES), 1) % R).astype(f32).astype(bf16)


def three(x, axis):
    high = x.astype(bf16).astype(f32)
    middle = (x - high).astype(bf16).astype(f32)
    low = (x - high) - middle
    return jnp.concatenate([high, middle, low, jnp.zeros_like(low)], axis=axis).astype(bf16)


def split(x):
    high = x.astype(bf16).astype(f32)
    return jnp.where(iota(x.shape, 1) < R, high, x - high).astype(bf16)


def join(x):
    return x[:, :R] + x[:, R:2 * R]


def send_form(gram, rhs, put):
    high = rhs.astype(bf16).astype(f32)
    parts = jnp.concatenate([high, rhs - high], axis=1).astype(bf16)
    return (gram + dot(parts, put)).astype(LINK)


def user_kernel(coords_in, counts, values_in, observed_in, items_in, weeks, table_in, out, mask, weighted, wpairs, wrows,
                table, places, coords, values, observed, items, ipairs, irows, gram, rhs, sems):
    moves = {}
    for n, (name, source, target) in enumerate((
        ("coords", coords_in, coords), ("table", table_in, table), ("items", items_in, items),
        ("observed0", observed_in.at[0], observed.at[0]), ("values0", values_in.at[0], values.at[0]),
        ("observed1", observed_in.at[1], observed.at[1]), ("values1", values_in.at[1], values.at[1]),
    )):
        moves[name] = pltpu.make_async_copy(source, target, sems.at[n])
        moves[name].start()
    gram[...] = jnp.zeros_like(gram)
    rhs[...] = jnp.zeros_like(rhs)
    for name in ("coords", "table", "items"):
        moves[name].wait()
    one, two, put = table[:R], table[R:2 * R], table[2 * R:]
    rows = three(items[...], 0)
    ipairs[...] = dot(rows, jnp.concatenate([one] * PACK), (0, 0)) * dot(rows, jnp.concatenate([two] * PACK), (0, 0))
    irows[...] = dot(rows, fold(), (0, 0))

    def block(slot):
        ubase = pl.multiple_of(coords[slot, 0] * B, B)
        ibase = pl.multiple_of(coords[slot, 1] * B, B)
        wpairs[slot], wrows[slot] = week_block(weeks, one, two, coords[slot, 2])
        own = observed[slot].astype(f32)
        mask[slot] = own.astype(bf16)
        weighted[slot] = (values[slot].astype(f32) * own).astype(bf16)
        wp = wpairs[slot].astype(f32)
        wr = wrows[slot].astype(f32)
        ip = ipairs[pl.ds(ibase, B), :]
        ir = irows[pl.ds(ibase, B), :]
        gram_add = jnp.zeros((B, WIDTH), f32)
        rhs_add = jnp.zeros((B, LANES), f32)
        for c in range(B // SIDE):
            here = slice(c * SIDE, (c + 1) * SIDE)
            cells = slice(c * CHUNK, (c + 1) * CHUNK)
            outer = (ip[here][:, None, :] * wp[None]).reshape(CHUNK, WIDTH).astype(bf16)
            gram_add += dot(mask[slot, :, cells], outer)
            outer = split((ir[here][:, None, :] * wr[None]).reshape(CHUNK, LANES))
            rhs_add += dot(weighted[slot, :, cells], outer)
        gram[pl.ds(ubase, B), :] += gram_add
        rhs[pl.ds(ubase, B), :] += join(rhs_add)

    moves["observed0"].wait()
    moves["values0"].wait()
    block(0)
    moves["observed1"].wait()
    moves["values1"].wait()

    @pl.when(counts[0, 0] > 1)
    def _():
        block(1)

    for slot in range(2):
        for n in range(2):
            places[slot, n] = coords[slot, n]
    places[0, 2] = counts[0, 0]
    places[1, 2] = counts[0, 0]
    out[...] = send_form(gram[...], rhs[...], put)


def item_kernel(places, mask, weighted, users, wpairs, wrows, table, out, gram, rhs):
    gram[...] = jnp.zeros_like(gram)
    rhs[...] = jnp.zeros_like(rhs)
    one, two, put = table[:R], table[R:2 * R], table[2 * R:]

    def block(slot):
        ubase = pl.multiple_of(places[slot, 0] * B, B)
        ibase = pl.multiple_of(places[slot, 1] * B, B)
        rows = users[pl.ds(ubase, B), :][:, :R]
        parts = three(rows, 1)
        upairs = dot(parts, jnp.concatenate([one] * PACK)) * dot(parts, jnp.concatenate([two] * PACK))
        upairs = upairs.astype(bf16)
        urows = split(jnp.concatenate([rows] * PACK, axis=1))
        wp = wpairs[slot].astype(f32)
        wr = wrows[slot].astype(f32)
        gram_add, rhs_add = [], []
        for c in range(B // SIDE):
            cells = slice(c * CHUNK, (c + 1) * CHUNK)
            cross = dot(mask[slot, :, cells], upairs, (0, 0)).reshape(SIDE, B, WIDTH)
            gram_add.append(jnp.sum(cross * wp[None], axis=1))
            moment = dot(weighted[slot, :, cells], urows, (0, 0)).reshape(SIDE, B, LANES)
            rhs_add.append(jnp.sum(moment * wr[None], axis=1))
        gram[pl.ds(ibase, B), :] += jnp.concatenate(gram_add, axis=0)
        rhs[pl.ds(ibase, B), :] += join(jnp.concatenate(rhs_add, axis=0))

    block(0)

    @pl.when(places[0, 2] > 1)
    def _():
        block(1)

    out[...] = send_form(gram[...], rhs[...], put)


def solve_kernel(parts, out, copies):
    count = parts.shape[0]
    pick = (iota((count, LANES), 0) % T == iota((count, LANES), 1)).astype(f32)
    if LINK == bf16:
        packed = dot(parts[...], pick.astype(bf16), (0, 0))
    else:
        packed = dot(parts[...], pick, (0, 0), precise)
    sub = iota((T, LANES), 0)

    def tile(r, t):
        first = START[r] + (t - r // T) * T
        return packed[first:first + T]

    def spread(x, n):
        return jnp.broadcast_to(x[n:n + 1], (T, LANES))

    tiles = R // T
    rows = {}
    for r in range(R):
        for t in range(r // T, tiles):
            x = tile(r, t)
            rows[r, t] = x + jnp.where(sub == r % T, ridge_weight, 0.0) if t == r // T else x
    side = []
    for j in range(tiles):
        row5, row6, row7 = (tile(j * T + n, j) for n in (5, 6, 7))
        high = jnp.where(sub == 7, spread(row6, 0), row7)
        low = jnp.where(sub == 0, row5, row6)
        low = jnp.where(sub == 6, spread(row5, 1), low)
        low = jnp.where(sub == 7, spread(row5, 2), low)
        side.append(high + low)
    factor, right = {}, []
    for k in range(R):
        own = k // T
        inverse = 1.0 / spread(rows[k, own], k % T)
        scaled = {t: rows[k, t] * inverse for t in range(own, tiles)}
        mine = spread(side[own], k % T)
        right.append(mine * inverse)
        for t in range(own, tiles):
            side[t] = side[t] - scaled[t] * mine
        for r in range(k + 1, R):
            factor[k, r] = spread(scaled[r // T], r % T)
            for t in range(r // T, tiles):
                rows[r, t] = rows[r, t] - factor[k, r] * rows[k, t]
    answer = []
    for s in range(R - 1, -1, -1):
        for k in range(s):
            right[k] = right[k] - factor[k, s] * right[s]
    for j in range(tiles):
        x = right[j * T]
        for n in range(1, T):
            x = jnp.where(sub == n, right[j * T + n], x)
        answer.append(x)
    answer = jnp.concatenate(answer + [jnp.zeros((LANES - R, LANES), f32)], axis=0)
    answer = jnp.transpose(answer)[:T]
    out[...] = answer[:, :R]
    copies[...] = jnp.broadcast_to(answer[None], copies.shape)


def vmem():
    return pl.BlockSpec(memory_space=pltpu.VMEM)


def smem():
    return pl.BlockSpec(memory_space=pltpu.SMEM)


def anywhere():
    return pl.BlockSpec(memory_space=pl.ANY)


PARAMS = pltpu.CompilerParams(vmem_limit_bytes=48 * 1024 * 1024)


def user_equations(coords, counts, values, observed, items, weeks, table):
    coords, values, observed, items, table = (
        pltpu.with_memory_space_constraint(x, pltpu.HBM) for x in (coords, values, observed, items, table)
    )
    return pl.pallas_call(
        user_kernel,
        out_shape=(
            pltpu.VMEM((UBD * B, WIDTH), LINK),
            pltpu.VMEM(values.shape, bf16),
            pltpu.VMEM(values.shape, bf16),
            pltpu.VMEM((2, B, WIDTH), bf16),
            pltpu.VMEM((2, B, LANES), bf16),
            pltpu.VMEM(table.shape, bf16),
            jax.ShapeDtypeStruct((2, 3), jnp.int32),
        ),
        in_specs=[anywhere(), smem()] + [anywhere()] * 3 + [vmem(), anywhere()],
        out_specs=[vmem()] * 6 + [smem()],
        scratch_shapes=[
            pltpu.SMEM(coords.shape, jnp.int32),
            pltpu.VMEM(values.shape, bf16), pltpu.VMEM(observed.shape, jnp.int32), pltpu.VMEM(items.shape, f32),
            pltpu.VMEM((IBD * B, WIDTH), f32), pltpu.VMEM((IBD * B, LANES), f32),
            pltpu.VMEM((UBD * B, WIDTH), f32), pltpu.VMEM((UBD * B, R), f32), pltpu.SemaphoreType.DMA((7,)),
        ],
        compiler_params=PARAMS,
    )(coords, counts, values, observed, items, weeks, table)


def item_equations(places, mask, weighted, users, wpairs, wrows, table):
    return pl.pallas_call(
        item_kernel,
        out_shape=pltpu.VMEM((IBD * B, WIDTH), LINK),
        in_specs=[smem()] + [vmem()] * 6,
        out_specs=vmem(),
        scratch_shapes=[pltpu.VMEM((IBD * B, WIDTH), f32), pltpu.VMEM((IBD * B, R), f32)],
        compiler_params=PARAMS,
    )(places, mask, weighted, users, wpairs, wrows, table)


def solve(parts, peers):
    return pl.pallas_call(
        solve_kernel,
        out_shape=(jax.ShapeDtypeStruct((T, R), f32), pltpu.VMEM((peers, T, LANES), f32)),
        in_specs=[vmem()],
        out_specs=(vmem(), vmem()),
        compiler_params=PARAMS,
    )(parts)


def copies_kernel(x, out):
    rows = x[...].reshape(out.shape[1:])
    out[...] = jnp.broadcast_to(rows[None], out.shape)


def copies_of(x, peers):
    return pl.pallas_call(
        copies_kernel,
        out_shape=pltpu.VMEM((peers, x.shape[0], LANES), x.dtype),
        in_specs=[vmem()],
        out_specs=vmem(),
        compiler_params=PARAMS,
    )(x)


def exchange(x, axis):
    return lax.all_to_all(x, axis, 0, 0, tiled=True)


def shards(values, observed, coords, counts, item_factors, week_factors):
    n_slab, n_fib = lax.axis_size("slab"), lax.axis_size("fib")
    packed = week_factors.astype(bf16).reshape(1, 1, LANES)
    weeks = exchange(jnp.broadcast_to(packed, (n_fib, 1, LANES)), "fib")
    weeks = exchange(copies_of(weeks, n_slab), "slab").reshape(n_slab * n_fib, LANES)
    parts, mask, weighted, wpairs, wrows, table, places = user_equations(
        coords[0], counts, values[0], observed[0], item_factors.T, weeks, jnp.asarray(TABLE, bf16)
    )
    user_out, copies = solve(exchange(parts, "fib"), n_fib)
    users = exchange(copies, "fib").reshape(UBD * B, LANES)
    parts = item_equations(places, mask, weighted, users, wpairs, wrows, table)
    _, copies = solve(exchange(parts, "slab"), n_slab)
    item_updated = exchange(copies, "slab").reshape(IBD * B, LANES)[:, :R]
    return (user_out, item_updated)


def solution(mesh):
    in_specs = (
        P("slab", "fib", None, None),
        P("slab", "fib", None, None),
        P("slab", "fib", None),
        P("slab", "fib"),
        P("fib", None),
        P(("slab", "fib"), None),
    )
    out_specs = (P(("slab", "fib"), None), P("fib", None))
    return jax.shard_map(shards, mesh=mesh, in_specs=in_specs, out_specs=out_specs, check_vma=False)
```

time: 132 us -> 112 us (0.85)
  local copies, waits for them, and re-layouts: 19.9 us -> 0.78 us
  other arithmetic: 3.5 us -> 0.68 us
  waiting for transfers between devices: 7.08 us -> 8.52 us
  Pallas kernels: 9.11 us -> 10.5 us
    unnamed x45 -> x1, local copies, waits for them, and re-layouts: 18.6 us -> 0.68 us
    all_to_all x2 -> x0, other arithmetic: 2.82 us -> none  [the longest x1 2.11 us: shards(): users = lax.all_to_all(copies, 'fib', 0, 0, tiled=True).reshape(UBD * B, R)]
    all_to_all x1, waiting for transfers between devices: 7.08 us -> 8.52 us  [exchange(): return lax.all_to_all(x, axis, 0, 0, tiled=True)]
    pallas_call x2 -> x3, Pallas kernels: 6.25 us -> 7.62 us  [the longest x1 3.95 us: user_equations(): pl.pallas_call(user_kernel, out_shape=(pltpu.VMEM((UBD * B, WIDTH), LINK)...]
  transfers between devices with their start and end apart: 1 -> 1, of which waited for: 1 -> 1; matrix products, arithmetic and copies ran while one was open for 1% -> 0% of each run, Pallas kernels for 0% -> 0%
where the time goes in v2:
time: 112 us; the launch traced here: 111 us
  blocking collectives  77.2 us (69%)
  starting transfers between devices  12.4 us (11%)
  Pallas kernels  10.5 us (9%)
  waiting for transfers between devices  8.52 us (8%)
  between operations  1.3 us (1%)
    all_to_all x5, blocking collectives, exchange(): return lax.all_to_all(x, axis, 0, 0, tiled=True)  77.2 us
    all_to_all x1, starting transfers between devices, exchange(): return lax.all_to_all(x, axis, 0, 0, tiled=True)  12.4 us
    all_to_all x1, waiting for transfers between devices, exchange(): return lax.all_to_all(x, axis, 0, 0, tiled=True)  8.52 us
    pallas_call x1, Pallas kernels, user_equations(): pl.pallas_call(user_kernel, out_shape=(pltpu.VMEM((UBD * B, WIDTH), LINK)...  3.95 us
    pallas_call x1, Pallas kernels, item_equations(): pl.pallas_call(item_kernel, out_shape=pltpu.VMEM((IBD * B, WIDTH), LINK),...  2.97 us
    pallas_call x2, Pallas kernels, solve(): pl.pallas_call(solve_kernel, out_shape=(jax.ShapeDtypeStruct((T, R), f32)...  2.86 us
  transfers between devices with their start and end apart: 1, of which 1 were waited for; matrix products, arithmetic and copies ran while one was open for 0% of the time, Pallas kernels for 0%

profile of v2, /device:TPU:1, one launch (start us, length us, event | category | flops | bytes accessed | tf_op | source)
XLA Modules:
  0.0 111.4 jit_solution(4988267022837779701)
XLA Ops:
  0.6 0.7 convert_element_type.3
  1.3 0.1 broadcast_in_dim.7
  1.4 18.9 %all_to_all.42.x = bf16[32,1,128]{2,1,0:T(2,128)(2,1)S(1)} all-to-all(bf16[32,1,128]{2,1,0:T(2,128)(2,1)S(1)} %broadcast_in_dim.8), channel_id=1, replica_groups=mesh['slab'=16,'fib'=32] {'fib'}, dimensions={0} | all-to-all | bytes 16384 | tf_op jit(solution)/shard_map/all_to_all | solution.py:335
  20.4 0.7 shard_map.86
  21.1 12.4 %all-to-all-start.1 = ((bf16[16,32,128]{2,1,0:T(8,128)(2,1)}), bf16[16,32,128]{2,1,0:T(8,128)(2,1)S(1)}, u32[]{:S(2)}, u32[]{:S(2)}) async-start(bf16[16,32,128]{2,1,0:T(8,128)(2,1)} %shard_map.86), calls=%async_computation.1 | async-start | bytes 262144 | tf_op jit(solution)/shard_map/all_to_all | solution.py:335
  34.1 8.5 %all-to-all-done.1 = bf16[16,32,128]{2,1,0:T(8,128)(2,1)S(1)} async-done(((bf16[16,32,128]{2,1,0:T(8,128)(2,1)}), bf16[16,32,128]{2,1,0:T(8,128)(2,1)S(1)}, u32[]{:S(2)}, u32[]{:S(2)}) %all-to-all-start.1) | async-done | bytes 131104 | tf_op jit(solution)/shard_map/all_to_all | solution.py:335
  42.7 3.9 %shard_map.87 = (bf16[256,640]{1,0:T(8,128)(2,1)S(1)}, bf16[2,64,4096]{2,1,0:T(8,128)(2,1)S(1)}, bf16[2,64,4096]{2,1,0:T(8,128)(2,1)S(1)}, bf16[2,64,640]{2,1,0:...) custom-call(s32[2,3]{1,0:T(2,128)} %bitcast.22, ...), custom_call_target="tpu_custom_call" | custom-call | tf_op jit(solution)/shard_map/pallas_call | solution.py:275
  46.6 15.8 %all_to_all.43 = bf16[32,8,640]{2,1,0:T(8,128)(2,1)S(1)} all-to-all(bf16[32,8,640]{2,1,0:T(8,128)(2,1)S(1)} %bitcast.17), channel_id=1, replica_groups=mesh['slab'=16,'fib'=32] {'fib'}, dimensions={0} | all-to-all | bytes 655360 | tf_op jit(solution)/shard_map/all_to_all | solution.py:335
  62.4 1.4 %shard_map.88 = (f32[8,32]{1,0:T(8,128)}, f32[32,8,128]{2,1,0:T(8,128)S(1)}) custom-call(bf16[256,640]{1,0:T(8,128)(2,1)S(1)} %bitcast.12), custom_call_target="tpu_custom_call" | custom-call | tf_op jit(solution)/shard_map/pallas_call | solution.py:310
  63.8 15.7 %all_to_all.44 = f32[32,8,128]{2,1,0:T(8,128)S(1)} all-to-all(f32[32,8,128]{2,1,0:T(8,128)S(1)} %get-tuple-element.17), channel_id=1, replica_groups=mesh['slab'=16,'fib'=32] {'fib'}, dimensions={0} | all-to-all | bytes 262144 | tf_op jit(solution)/shard_map/all_to_all | solution.py:335
  79.5 3.0 %shard_map.89 = bf16[128,640]{1,0:T(8,128)(2,1)S(1)} custom-call(s32[2,3]{1,0:T(2,128)S(1)} %get-tuple-element.14.places, bf16[2,64,4096]{2,1,0:T(8,128)(2,1)S(1)} %get-tuple-element.15.mask, bf16[2,64,4096]{2,1,0:T(8,128)(2,1)S(1)} %get-tuple-element.16.weighted, f32[256,128]{1,0:T(8,128)S(1)} %bitcast.16, ...), custom_call_target="tpu_custom_call" | custom-call | tf_op jit(solution)/shard_map/pallas_call | solution.py:299
  82.5 16.6 %all_to_all.45 = bf16[16,8,640]{2,1,0:T(8,128)(2,1)S(1)} all-to-all(bf16[16,8,640]{2,1,0:T(8,128)(2,1)S(1)} %bitcast.13), channel_id=1, replica_groups=mesh['slab'=16,'fib'=32] {'slab'}, dimensions={0} | all-to-all | bytes 327680 | tf_op jit(solution)/shard_map/all_to_all | solution.py:335
  99.0 1.4 %shard_map.90 = (f32[8,32]{1,0:T(8,128)}, f32[16,8,128]{2,1,0:T(8,128)S(1)}) custom-call(bf16[128,640]{1,0:T(8,128)(2,1)S(1)} %bitcast.14), custom_call_target="tpu_custom_call" | custom-call | tf_op jit(solution)/shard_map/pallas_call | solution.py:310
  100.4 10.2 %all_to_all.46 = f32[16,8,128]{2,1,0:T(8,128)S(1)} all-to-all(f32[16,8,128]{2,1,0:T(8,128)S(1)} %get-tuple-element.21), channel_id=1, replica_groups=mesh['slab'=16,'fib'=32] {'slab'}, dimensions={0} | all-to-all | bytes 131072 | tf_op jit(solution)/shard_map/all_to_all | solution.py:335
  110.7 0.7 copy.10
  (1 shorter events, 0.0 us)
Async XLA Ops:
  21.1 21.6 %all-to-all-start.1 = ((bf16[16,32,128]{2,1,0:T(8,128)(2,1)}), bf16[16,32,128]{2,1,0:T(8,128)(2,1)S(1)}, u32[]{:S(2)}, u32[]{:S(2)}) async-start(bf16[16,32,128]{2,1,0:T(8,128)(2,1)} %shard_map.86), calls=%async_computation.1 | async-start | bytes 262144 | tf_op jit(solution)/shard_map/all_to_all | solution.py:335

commit v3 on v2

v3 whole, which is shorter than its diff:
```python
import jax
import jax.numpy as jnp
import numpy as np
from jax import lax
from jax.experimental import pallas as pl
from jax.experimental.pallas import tpu as pltpu
from jax.sharding import PartitionSpec as P

B = 64
R = 32
UBD = 4
IBD = 2
T = 8
LANES = 128
SIDE = 4
CHUNK = SIDE * B
PACK = LANES // R
WROWS = B // PACK
FIB = 32
SLABS, FIBS = ("z", "core"), ("x", "y")
ridge_weight = 1.0
precise = lax.Precision.HIGHEST
LINK = jnp.bfloat16
f32 = jnp.float32
bf16 = jnp.bfloat16


def tables():
    start, left, right = {}, [], []
    for r in range(R):
        start[r] = len(left)
        for s in range(r // T * T, R):
            left.append(r)
            right.append(s)
    width = len(left)
    one = np.zeros((R, width), np.float32)
    two = np.zeros((R, width), np.float32)
    for k, (r, s) in enumerate(zip(left, right)):
        if s >= r:
            one[r, k] = 1
            two[s, k] = 1
    put = np.zeros((LANES, width), np.float32)
    for j in range(R // T):
        row5, row6, row7 = (start[j * T + n] for n in (5, 6, 7))
        for n in range(7):
            put[j * T + n, row7 + n] = 1
        put[j * T + 7, row6] = 1
        for n in range(1, 6):
            put[R + j * T + n, row6 + n] = 1
        put[R + j * T, row5] = 1
        put[R + j * T + 6, row5 + 1] = 1
        put[R + j * T + 7, row5 + 2] = 1
    return start, width, one, two, put


START, WIDTH, ONE, TWO, PUT = tables()
TABLE = np.concatenate([ONE, TWO, PUT[:2 * R]])


def dot(a, b, dims=(1, 0), precision=None):
    return lax.dot_general(
        a, b, (((dims[0],), (dims[1],)), ((), ())), preferred_element_type=f32, precision=precision
    )


def iota(shape, dim):
    return lax.broadcasted_iota(jnp.int32, shape, dim)


def week_block(weeks, one, two, start):
    slab, part = start // (FIB // WROWS), start % (FIB // WROWS)
    both = weeks[pl.ds(slab // 2 * FIB + part * WROWS, WROWS)].astype(f32)
    packed = jnp.where(slab % 2 == 0, both[:, 0], both[:, 1]).astype(bf16)
    spread = (iota((B, WROWS), 0) // PACK == iota((B, WROWS), 1)).astype(f32).astype(bf16)
    rows = dot(spread, packed)
    own = iota((B, LANES), 0) % PACK == iota((B, LANES), 1) // R
    rows = jnp.where(own, rows, 0.0).astype(bf16)
    pairs = dot(rows, jnp.concatenate([one] * PACK)) * dot(rows, jnp.concatenate([two] * PACK))
    return pairs.astype(bf16), dot(rows, fold()).astype(bf16)


def unfold(x):
    return sum(x[:, n * R:(n + 1) * R] for n in range(PACK))


def fold():
    return (iota((LANES, LANES), 0) % R == iota((LANES, LANES), 1) % R).astype(f32).astype(bf16)


def three(x, axis):
    high = x.astype(bf16).astype(f32)
    middle = (x - high).astype(bf16).astype(f32)
    low = (x - high) - middle
    return jnp.concatenate([high, middle, low, jnp.zeros_like(low)], axis=axis).astype(bf16)


def send_form(gram, rhs, put):
    high = rhs.astype(bf16).astype(f32)
    parts = jnp.concatenate([high, rhs - high], axis=1).astype(bf16)
    return (gram + dot(parts, put)).astype(LINK)


def turn(own, strips, turned, slot):
    pairs = B // 2
    for t in range(pairs):
        strips[t * B:(t + 1) * B] = own[:, t * LANES:(t + 1) * LANES]
    first = iota((pairs, LANES), 1) < B
    for v in range(pairs):
        a, b = (strips[pl.ds(2 * v + n, pairs, stride=B)] for n in range(2))
        even = jnp.where(first, a, pltpu.roll(b, B, 1))
        odd = jnp.where(first, pltpu.roll(a, B, 1), b)
        turned[slot, :, v * LANES:(v + 1) * LANES] = jnp.concatenate([even, odd]).astype(bf16)


def item_at(rows, dim):
    place = iota(rows, dim) % B
    return iota(rows, dim) // B * B + place % (B // 2) * 2 + place // (B // 2)


def paired(mask, slot, pairs, wp):
    total = jnp.zeros((B, WIDTH), f32)
    for c in range(B // SIDE):
        outer = []
        for i in range(c * SIDE, (c + 1) * SIDE):
            row = jnp.broadcast_to(pairs[i:i + 1], (16, WIDTH)).astype(bf16)
            outer.append((wp * row[None]).reshape(B, WIDTH))
        total += dot(mask[slot, :, c * CHUNK:(c + 1) * CHUNK], jnp.concatenate(outer))
    return total


def prepare_kernel(coords_in, counts, values_in, observed_in, items_in, table_in, mask, turned, weighted, ipairs, irows,
                   table, places, coords, values, observed, items, strips, sems):
    moves = []
    for n, (source, target) in enumerate((
        (table_in, table), (items_in, items), (observed_in.at[0], observed.at[0]), (values_in.at[0], values.at[0]),
        (observed_in.at[1], observed.at[1]), (values_in.at[1], values.at[1]), (coords_in, coords),
    )):
        moves.append(pltpu.make_async_copy(source, target, sems.at[n]))
        moves[n].start()
    moves[0].wait()
    moves[1].wait()
    rows = three(items[...], 0)
    ipairs[...] = dot(rows, jnp.concatenate([table[:R]] * PACK), (0, 0)) * dot(
        rows, jnp.concatenate([table[R:2 * R]] * PACK), (0, 0)
    )
    irows[...] = dot(rows, fold(), (0, 0))
    for slot in range(2):
        moves[2 + 2 * slot].wait()
        moves[3 + 2 * slot].wait()
        own = observed[slot].astype(f32)
        mask[slot] = own.astype(bf16)
        weighted[slot] = (values[slot].astype(f32) * own).astype(bf16)
        turn(own, strips, turned, slot)
    moves[6].wait()
    for slot in range(2):
        for n in range(3):
            places[slot, n] = coords[slot, n]
        places[slot, 3] = counts[0, 0]


def user_kernel(places, weeks, mask, weighted, ipairs, irows, table, out, wpairs, moment, gram, rhs):
    gram[...] = jnp.zeros_like(gram)
    rhs[...] = jnp.zeros_like(rhs)
    one, two, put = table[:R], table[R:2 * R], table[2 * R:]

    def block(slot):
        ubase = pl.multiple_of(places[slot, 0] * B, B)
        ibase = pl.multiple_of(places[slot, 1] * B, B)
        wp, wr = week_block(weeks, one, two, places[slot, 2])
        wpairs[slot] = wp
        gram[pl.ds(ubase, B), :] += paired(mask, slot, ipairs[pl.ds(ibase, B), :], wp.reshape(B // 16, 16, WIDTH))
        ir = irows[pl.ds(ibase, B), :]
        lane = iota((1, LANES), 1) // R
        apart = iota((CHUNK, LANES), 0) // B == iota((CHUNK, LANES), 1) // R
        apart = jnp.where(apart, jnp.concatenate([wr.astype(f32)] * SIDE), 0.0).astype(bf16)
        rhs_add = jnp.zeros((B, LANES), f32)
        for c in range(B // SIDE):
            here = dot(weighted[slot, :, c * CHUNK:(c + 1) * CHUNK], apart)
            moment[slot, c] = here
            row = sum(jnp.where(lane == n, ir[c * SIDE + n:c * SIDE + n + 1], 0.0) for n in range(SIDE))
            rhs_add += here * row
        rhs[pl.ds(ubase, B), :] += unfold(rhs_add)

    block(0)

    @pl.when(places[0, 3] > 1)
    def _():
        block(1)

    out[...] = send_form(gram[...], rhs[...], put)


def item_kernel(places, turned, moment, users, wpairs, table, out, gram, rhs):
    gram[...] = jnp.zeros_like(gram)
    rhs[...] = jnp.zeros_like(rhs)
    one, two, put = table[:R], table[R:2 * R], table[2 * R:]

    def block(slot):
        ubase = pl.multiple_of(places[slot, 0] * B, B)
        ibase = pl.multiple_of(places[slot, 1] * B, B)
        rows = users[pl.ds(ubase, B), :][:, :R]
        parts = three(rows, 1)
        upairs = dot(parts, jnp.concatenate([one] * PACK)) * dot(parts, jnp.concatenate([two] * PACK))
        gram[pl.ds(ibase, B), :] += paired(turned, slot, upairs, wpairs[slot].reshape(B // 16, 16, WIDTH))
        urows = jnp.concatenate([rows] * PACK, axis=1)
        sums = three(jnp.sum(moment[slot] * urows[None], axis=1), 0)
        spread = iota((B, B), 1) % (B // SIDE) == item_at((B, B), 0) // SIDE
        sums = dot(jnp.where(spread, 1.0, 0.0).astype(bf16), sums)
        sums = jnp.where(item_at(sums.shape, 0) % SIDE == iota(sums.shape, 1) // R, sums, 0.0)
        rhs[pl.ds(ibase, B), :] += unfold(sums)

    block(0)

    @pl.when(places[0, 3] > 1)
    def _():
        block(1)

    count = IBD * B
    order = jnp.where(item_at((count, count), 1) == iota((count, count), 0), 1.0, 0.0).astype(bf16)
    out[...] = dot(order, send_form(gram[...], rhs[...], put)).astype(LINK)


def solve_kernel(parts, out, copies):
    count = parts.shape[0]
    pick = (iota((count, LANES), 0) % T == iota((count, LANES), 1)).astype(f32)
    if LINK == bf16:
        packed = dot(parts[...], pick.astype(bf16), (0, 0))
    else:
        packed = dot(parts[...], pick, (0, 0), precise)
    sub = iota((T, LANES), 0)

    def tile(r, t):
        first = START[r] + (t - r // T) * T
        return packed[first:first + T]

    def spread(x, n):
        return jnp.broadcast_to(x[n:n + 1], (T, LANES))

    tiles = R // T
    rows = {}
    for r in range(R):
        for t in range(r // T, tiles):
            x = tile(r, t)
            rows[r, t] = x + jnp.where(sub == r % T, ridge_weight, 0.0) if t == r // T else x
    side = []
    for j in range(tiles):
        row5, row6, row7 = (tile(j * T + n, j) for n in (5, 6, 7))
        high = jnp.where(sub == 7, spread(row6, 0), row7)
        low = jnp.where(sub == 0, row5, row6)
        low = jnp.where(sub == 6, spread(row5, 1), low)
        low = jnp.where(sub == 7, spread(row5, 2), low)
        side.append(high + low)
    factor, right = {}, []
    for k in range(R):
        own = k // T
        inverse = 1.0 / spread(rows[k, own], k % T)
        scaled = {t: rows[k, t] * inverse for t in range(own, tiles)}
        mine = spread(side[own], k % T)
        right.append(mine * inverse)
        for t in range(own, tiles):
            side[t] = side[t] - scaled[t] * mine
        for r in range(k + 1, R):
            factor[k, r] = spread(scaled[r // T], r % T)
            for t in range(r // T, tiles):
                rows[r, t] = rows[r, t] - factor[k, r] * rows[k, t]
    answer = []
    for s in range(R - 1, -1, -1):
        for k in range(s):
            right[k] = right[k] - factor[k, s] * right[s]
    for j in range(tiles):
        x = right[j * T]
        for n in range(1, T):
            x = jnp.where(sub == n, right[j * T + n], x)
        answer.append(x)
    answer = jnp.concatenate(answer + [jnp.zeros((LANES - R, LANES), f32)], axis=0)
    answer = jnp.transpose(answer)[:T]
    out[...] = answer[:, :R]
    copies[...] = jnp.broadcast_to(answer[None], copies.shape)


def vmem():
    return pl.BlockSpec(memory_space=pltpu.VMEM)


def smem():
    return pl.BlockSpec(memory_space=pltpu.SMEM)


def anywhere():
    return pl.BlockSpec(memory_space=pl.ANY)


def params(mib):
    return pltpu.CompilerParams(vmem_limit_bytes=mib * 1024 * 1024)


def prepare(coords, counts, values, observed, items, table):
    coords, values, observed, items, table = (
        pltpu.with_memory_space_constraint(x, pltpu.HBM) for x in (coords, values, observed, items, table)
    )
    return pl.pallas_call(
        prepare_kernel,
        out_shape=(
            pltpu.VMEM(values.shape, bf16),
            pltpu.VMEM(values.shape, bf16),
            pltpu.VMEM(values.shape, bf16),
            pltpu.VMEM((IBD * B, WIDTH), f32),
            pltpu.VMEM((IBD * B, LANES), f32),
            pltpu.VMEM(table.shape, bf16),
            jax.ShapeDtypeStruct((2, 4), jnp.int32),
        ),
        in_specs=[anywhere(), smem()] + [anywhere()] * 4,
        out_specs=[vmem()] * 6 + [smem()],
        scratch_shapes=[
            pltpu.SMEM(coords.shape, jnp.int32), pltpu.VMEM(values.shape, bf16), pltpu.VMEM(observed.shape, jnp.int32), pltpu.VMEM(items.shape, f32),
            pltpu.VMEM((B * B // 2, LANES), f32), pltpu.SemaphoreType.DMA((7,)),
        ],
        compiler_params=params(16),
    )(coords, counts, values, observed, items, table)


def user_equations(places, weeks, mask, weighted, ipairs, irows, table):
    return pl.pallas_call(
        user_kernel,
        out_shape=(
            pltpu.VMEM((UBD * B, WIDTH), LINK),
            pltpu.VMEM((2, B, WIDTH), bf16),
            pltpu.VMEM((2, B // SIDE, B, LANES), f32),
        ),
        in_specs=[smem()] + [vmem()] * 6,
        out_specs=[vmem()] * 3,
        scratch_shapes=[pltpu.VMEM((UBD * B, WIDTH), f32), pltpu.VMEM((UBD * B, R), f32)],
        compiler_params=params(16),
    )(places, weeks, mask, weighted, ipairs, irows, table)


def item_equations(places, turned, moment, users, wpairs, table):
    return pl.pallas_call(
        item_kernel,
        out_shape=pltpu.VMEM((IBD * B, WIDTH), LINK),
        in_specs=[smem()] + [vmem()] * 5,
        out_specs=vmem(),
        scratch_shapes=[pltpu.VMEM((IBD * B, WIDTH), f32), pltpu.VMEM((IBD * B, R), f32)],
        compiler_params=params(16),
    )(places, turned, moment, users, wpairs, table)


def solve(parts, peers):
    return pl.pallas_call(
        solve_kernel,
        out_shape=(jax.ShapeDtypeStruct((T, R), f32), pltpu.VMEM((peers, T, LANES), f32)),
        in_specs=[vmem()],
        out_specs=(vmem(), vmem()),
        compiler_params=params(16),
    )(parts)


def week_kernel(weeks, out):
    rows = weeks[...]
    row = jnp.concatenate([
        jnp.concatenate([rows[k * PACK + n:k * PACK + n + 1] for n in range(PACK)], axis=1) for k in range(2)
    ], axis=0)
    out[...] = jnp.broadcast_to(row[None], out.shape).astype(bf16)


def week_copies(weeks, peers):
    return pl.pallas_call(
        week_kernel,
        out_shape=pltpu.VMEM((peers, 2, LANES), bf16),
        in_specs=[vmem()],
        out_specs=vmem(),
        compiler_params=params(16),
    )(weeks)


def copies_kernel(x, out):
    rows = x[...].reshape(out.shape[1:])
    out[...] = jnp.broadcast_to(rows[None], out.shape)


def copies_of(x, peers):
    return pl.pallas_call(
        copies_kernel,
        out_shape=pltpu.VMEM((peers, x.shape[0], LANES), x.dtype),
        in_specs=[vmem()],
        out_specs=vmem(),
        compiler_params=params(16),
    )(x)


def exchange(x, axis):
    return lax.all_to_all(x, axis, 0, 0, tiled=True)


def shards(values, observed, coords, counts, item_factors, week_factors):
    n_slab, n_fib = lax.axis_size(SLABS), lax.axis_size(FIBS)
    pair = lax.all_gather(week_factors, "core", axis=0, tiled=True)
    copies = week_copies(pair, n_slab * n_fib // 2)
    weeks = exchange(copies, ("z", "x", "y"))
    mask, turned, weighted, ipairs, irows, table, places = prepare(
        coords[0], counts, values[0], observed[0], item_factors.T, jnp.asarray(TABLE, bf16)
    )
    parts, wpairs, moment = user_equations(places, weeks, mask, weighted, ipairs, irows, table)
    user_out, copies = solve(exchange(parts, FIBS), n_fib)
    users = exchange(copies, FIBS).reshape(UBD * B, LANES)
    parts = item_equations(places, turned, moment, users, wpairs, table)
    _, copies = solve(exchange(parts, SLABS), n_slab)
    item_updated = exchange(copies, SLABS).reshape(IBD * B, LANES)[:, :R]
    return (user_out, item_updated)


def solution(mesh):
    fine = jax.sharding.Mesh(mesh.devices.reshape(8, 2, 4, 8), SLABS + FIBS)
    in_specs = (
        P(SLABS, FIBS, None, None),
        P(SLABS, FIBS, None, None),
        P(SLABS, FIBS, None),
        P(SLABS, FIBS),
        P(FIBS, None),
        P(SLABS + FIBS, None),
    )
    out_specs = (P(SLABS + FIBS, None), P(FIBS, None))
    return jax.shard_map(shards, mesh=fine, in_specs=in_specs, out_specs=out_specs, check_vma=False)
```

time: 112 us -> 108 us (0.964)
  blocking collectives: 77.2 us -> 67.6 us
  starting transfers between devices: 12.4 us -> 17 us
  Pallas kernels: 10.5 us -> 12.4 us
  waiting for transfers between devices: 8.52 us -> 6.84 us
  local copies, waits for them, and re-layouts: 0.78 us -> 2.37 us
    all_to_all x5 -> x4, blocking collectives: 77.2 us -> 59.1 us  [exchange(): return lax.all_to_all(x, axis, 0, 0, tiled=True)]
    all_gather x0 -> x1, blocking collectives: none -> 8.49 us  [shards(): pair = lax.all_gather(week_factors, 'core', axis=0, tiled=True)]
    all_to_all x1, starting transfers between devices: 12.4 us -> 17 us  [exchange(): return lax.all_to_all(x, axis, 0, 0, tiled=True)]
    pallas_call x1 -> x2, Pallas kernels: 0.7 us -> 4.86 us  [the longest x1 4.07 us: prepare(): pl.pallas_call(prepare_kernel, out_shape=(pltpu.VMEM(values.shape, bf16),...]
    unnamed x1 -> x5, local copies, waits for them, and re-layouts: 0.68 us -> 2.37 us
    all_to_all x1, waiting for transfers between devices: 8.52 us -> 6.84 us  [exchange(): return lax.all_to_all(x, axis, 0, 0, tiled=True)]
    pallas_call x1, Pallas kernels: 3.95 us -> 2.36 us  [user_equations(): pl.pallas_call(user_kernel, out_shape=(pltpu.VMEM((UBD * B, WIDTH), LINK)...]
  transfers between devices with their start and end apart: 1 -> 1, of which waited for: 1 -> 1; matrix products, arithmetic and copies ran while one was open for 0% -> 0% of each run, Pallas kernels for 0% -> 4%
where the time goes in v3:
time: 108 us
  blocking collectives  67.6 us (63%)
  starting transfers between devices  17 us (16%)
  Pallas kernels  12.4 us (11%)
  waiting for transfers between devices  6.84 us (6%)
  local copies, waits for them, and re-layouts  2.37 us (2%)
  between operations  1.32 us (1%)
    all_to_all x4, blocking collectives, exchange(): return lax.all_to_all(x, axis, 0, 0, tiled=True)  59.1 us
    all_to_all x1, starting transfers between devices, exchange(): return lax.all_to_all(x, axis, 0, 0, tiled=True)  17 us
    all_gather x1, blocking collectives, shards(): pair = lax.all_gather(week_factors, 'core', axis=0, tiled=True)  8.49 us
    all_to_all x1, waiting for transfers between devices, exchange(): return lax.all_to_all(x, axis, 0, 0, tiled=True)  6.84 us
    pallas_call x1, Pallas kernels, prepare(): pl.pallas_call(prepare_kernel, out_shape=(pltpu.VMEM(values.shape, bf16),...  4.07 us
    pallas_call x2, Pallas kernels, solve(): pl.pallas_call(solve_kernel, out_shape=(jax.ShapeDtypeStruct((T, R), f32)...  2.86 us
    unnamed x5, local copies, waits for them, and re-layouts  2.37 us
    pallas_call x1, Pallas kernels, item_equations(): pl.pallas_call(item_kernel, out_shape=pltpu.VMEM((IBD * B, WIDTH), LINK),...  2.37 us
  transfers between devices with their start and end apart: 1, of which 1 were waited for; matrix products, arithmetic and copies ran while one was open for 0% of the time, Pallas kernels for 4%

profile of v3, /device:TPU:1, one launch (start us, length us, event | category | flops | bytes accessed | tf_op | source)
XLA Modules:
  0.0 107.5 jit_solution(1220087216674697626)
XLA Ops:
  0.6 8.5 %all-gather = f32[2,4,32]{2,1,0:T(4,128)S(1)} all-gather(f32[1,4,32]{2,1,0:T(4,128)} %bitcast.23), channel_id=1, replica_groups=mesh['z'=8,'core'=2,'x'=4,'y'=8] {'core'}, dimensions={0}, use_global_device_ids=true | all-gather | bytes 1536 | tf_op jit(solution)/shard_map/all_gather | solution.py:397
  9.1 0.8 shard_map.87
  9.9 17.0 %all-to-all-start = ((bf16[256,2,128]{2,1,0:T(2,128)(2,1)}), bf16[256,2,128]{2,1,0:T(2,128)(2,1)S(1)}, u32[]{:S(2)}, u32[]{:S(2)}) async-start(bf16[256,2,128]{2,1,0:T(2,128)(2,1)} %shard_map.87), calls=%async_computation | async-start | bytes 262144 | tf_op jit(solution)/shard_map/all_to_all | solution.py:392
  27.6 4.1 %shard_map.86 = (bf16[2,64,4096]{2,1,0:T(8,128)(2,1)S(1)}, bf16[2,64,4096]{2,1,0:T(8,128)(2,1)S(1)}, bf16[2,64,4096]{2,1,0:T(8,128)(2,1)S(1)}, f32[128,640]{1,0:...) custom-call(s32[2,3]{1,0:T(2,128)} %bitcast.24, s32[1,1]{1,0:T(1,128)S(6)} %copy.12.counts, ...), custom_call_target="tpu_custom_call" | custom-call | tf_op jit(solution)/shard_map/pallas_call | solution.py:301
  31.6 0.0 copy-start
  31.6 0.7 copy-done
  32.4 6.8 %all-to-all-done.weeks = bf16[256,2,128]{2,1,0:T(2,128)(2,1)S(1)} async-done(((bf16[256,2,128]{2,1,0:T(2,128)(2,1)}), bf16[256,2,128]{2,1,0:T(2,128)(2,1)S(1)}, u32[]{:S(2)}, u32[]{:S(2)}) %all-to-all-start) | async-done | bytes 131104 | tf_op jit(solution)/shard_map/all_to_all | solution.py:392
  39.2 0.0 copy-start.1
  39.2 1.0 copy-done.1
  40.2 2.4 %shard_map.88 = (bf16[256,640]{1,0:T(8,128)(2,1)S(1)}, bf16[2,64,640]{2,1,0:T(8,128)(2,1)S(1)}, f32[2,16,64,128]{3,2,1,0:T(8,128)S(1)}) custom-call(s32[2,4]{1,0:T(2,128)S(1)} %get-tuple-element.15.places, bf16[256,2,128]{2,1,0:T(2,128)(2,1)S(1)} %all-to-all-done.weeks, bf16[2,64,4096]{2,1,0:T(8,128)(2,1)S(1)} %get-tuple-element.16.mask, ...), custom_call_target="tpu_custom_call" | custom-call | tf_op jit(solution)/shard_map/pallas_call | solution.py:323
  42.6 14.7 %all_to_all.37 = bf16[32,8,640]{2,1,0:T(8,128)(2,1)S(1)} all-to-all(bf16[32,8,640]{2,1,0:T(8,128)(2,1)S(1)} %bitcast.17), channel_id=1, replica_groups=mesh['z'=8,'core'=2,'x'=4,'y'=8] {'x','y'}, dimensions={0} | all-to-all | bytes 655360 | tf_op jit(solution)/shard_map/all_to_all | solution.py:392
  57.2 1.4 %shard_map.89 = (f32[8,32]{1,0:T(8,128)}, f32[32,8,128]{2,1,0:T(8,128)S(1)}) custom-call(bf16[256,640]{1,0:T(8,128)(2,1)S(1)} %bitcast.13), custom_call_target="tpu_custom_call" | custom-call | tf_op jit(solution)/shard_map/pallas_call | solution.py:349
  58.7 15.8 %all_to_all.38 = f32[32,8,128]{2,1,0:T(8,128)S(1)} all-to-all(f32[32,8,128]{2,1,0:T(8,128)S(1)} %get-tuple-element.25), channel_id=1, replica_groups=mesh['z'=8,'core'=2,'x'=4,'y'=8] {'x','y'}, dimensions={0} | all-to-all | bytes 262144 | tf_op jit(solution)/shard_map/all_to_all | solution.py:392
  74.4 2.4 %shard_map.90 = bf16[128,640]{1,0:T(8,128)(2,1)S(1)} custom-call(s32[2,4]{1,0:T(2,128)S(1)} %get-tuple-element.15.places, bf16[2,64,4096]{2,1,0:T(8,128)(2,1)S(1)} %get-tuple-element.23.turned, f32[2,16,64,128]{3,2,1,0:T(8,128)S(1)} %get-tuple-element.24.moment, f32[256,128]{1,0:T(8,128)S(1)} %bitcast.16, bf16[2,64,640]{2,1,0:T(8,128)(2,1)S(1)} %get-tuple-element.26.wpairs, ...), custom_call_target="tpu_custom_call" | custom-call | tf_op jit(solution)/shard_map/pallas_call | solution.py:338
  76.8 18.2 %all_to_all.39 = bf16[16,8,640]{2,1,0:T(8,128)(2,1)S(1)} all-to-all(bf16[16,8,640]{2,1,0:T(8,128)(2,1)S(1)} %bitcast.14), channel_id=1, replica_groups=mesh['z'=8,'core'=2,'x'=4,'y'=8] {'z','core'}, dimensions={0} | all-to-all | bytes 327680 | tf_op jit(solution)/shard_map/all_to_all | solution.py:392
  95.0 1.4 %shard_map.91 = (f32[8,32]{1,0:T(8,128)}, f32[16,8,128]{2,1,0:T(8,128)S(1)}) custom-call(bf16[128,640]{1,0:T(8,128)(2,1)S(1)} %bitcast.15), custom_call_target="tpu_custom_call" | custom-call | tf_op jit(solution)/shard_map/pallas_call | solution.py:349
  96.4 10.4 %all_to_all.40 = f32[16,8,128]{2,1,0:T(8,128)S(1)} all-to-all(f32[16,8,128]{2,1,0:T(8,128)S(1)} %get-tuple-element.27), channel_id=1, replica_groups=mesh['z'=8,'core'=2,'x'=4,'y'=8] {'z','core'}, dimensions={0} | all-to-all | bytes 131072 | tf_op jit(solution)/shard_map/all_to_all | solution.py:392
  106.8 0.7 copy.11
Async XLA Ops:
  9.9 29.3 %all-to-all-start = ((bf16[256,2,128]{2,1,0:T(2,128)(2,1)}), bf16[256,2,128]{2,1,0:T(2,128)(2,1)S(1)}, u32[]{:S(2)}, u32[]{:S(2)}) async-start(bf16[256,2,128]{2,1,0:T(2,128)(2,1)} %shard_map.87), calls=%async_computation | async-start | bytes 262144 | tf_op jit(solution)/shard_map/all_to_all | solution.py:392
  31.6 0.7 copy-start
  39.2 1.0 copy-start.1

commit v4 on v3

--- a/solution.py
+++ b/solution.py
@@ -119,20 +119,21 @@
 
 def paired(mask, slot, pairs, wp):
     total = jnp.zeros((B, WIDTH), f32)
-    for c in range(B // SIDE):
+    step = 2 * SIDE
+    for c in range(0, B, step):
         outer = []
-        for i in range(c * SIDE, (c + 1) * SIDE):
+        for i in range(c, c + step):
             row = jnp.broadcast_to(pairs[i:i + 1], (16, WIDTH)).astype(bf16)
             outer.append((wp * row[None]).reshape(B, WIDTH))
-        total += dot(mask[slot, :, c * CHUNK:(c + 1) * CHUNK], jnp.concatenate(outer))
+        total += dot(mask[slot, :, c * B:(c + step) * B], jnp.concatenate(outer))
     return total
 
 
-def prepare_kernel(coords_in, counts, values_in, observed_in, items_in, table_in, mask, turned, weighted, ipairs, irows,
+def prepare_kernel(coords_in, counts, values_in, observed_in, items_in, table_in, mask, turned, weighted, irows,
                    table, places, coords, values, observed, items, strips, sems):
     moves = []
     for n, (source, target) in enumerate((
-        (table_in, table), (items_in, items), (observed_in.at[0], observed.at[0]), (values_in.at[0], values.at[0]),
+        (table_in, table.at[:TABLE.shape[0]]), (items_in, items), (observed_in.at[0], observed.at[0]), (values_in.at[0], values.at[0]),
         (observed_in.at[1], observed.at[1]), (values_in.at[1], values.at[1]), (coords_in, coords),
     )):
         moves.append(pltpu.make_async_copy(source, target, sems.at[n]))
@@ -140,9 +141,9 @@
     moves[0].wait()
     moves[1].wait()
     rows = three(items[...], 0)
-    ipairs[...] = dot(rows, jnp.concatenate([table[:R]] * PACK), (0, 0)) * dot(
-        rows, jnp.concatenate([table[R:2 * R]] * PACK), (0, 0)
-    )
+    pairs = dot(rows, jnp.concatenate([table[:R]] * PACK), (0, 0))
+    pairs *= dot(rows, jnp.concatenate([table[R:2 * R]] * PACK), (0, 0))
+    table[TABLE.shape[0]:] = pairs.astype(bf16)
     irows[...] = dot(rows, fold(), (0, 0))
     for slot in range(2):
         moves[2 + 2 * slot].wait()
@@ -158,24 +159,26 @@
         places[slot, 3] = counts[0, 0]
 
 
-def user_kernel(places, weeks, mask, weighted, ipairs, irows, table, out, wpairs, moment, gram, rhs):
+def user_kernel(places, weeks, mask, weighted, irows, table, out, wpairs, moment, gram, rhs):
     gram[...] = jnp.zeros_like(gram)
     rhs[...] = jnp.zeros_like(rhs)
-    one, two, put = table[:R], table[R:2 * R], table[2 * R:]
+    one, two, put = table[:R], table[R:2 * R], table[2 * R:TABLE.shape[0]]
 
     def block(slot):
         ubase = pl.multiple_of(places[slot, 0] * B, B)
         ibase = pl.multiple_of(places[slot, 1] * B, B)
         wp, wr = week_block(weeks, one, two, places[slot, 2])
         wpairs[slot] = wp
-        gram[pl.ds(ubase, B), :] += paired(mask, slot, ipairs[pl.ds(ibase, B), :], wp.reshape(B // 16, 16, WIDTH))
+        gram[pl.ds(ubase, B), :] += paired(mask, slot, table[pl.ds(pl.multiple_of(TABLE.shape[0] + ibase, B), B), :].astype(f32), wp.reshape(B // 16, 16, WIDTH))
         ir = irows[pl.ds(ibase, B), :]
         lane = iota((1, LANES), 1) // R
         apart = iota((CHUNK, LANES), 0) // B == iota((CHUNK, LANES), 1) // R
         apart = jnp.where(apart, jnp.concatenate([wr.astype(f32)] * SIDE), 0.0).astype(bf16)
         rhs_add = jnp.zeros((B, LANES), f32)
+        every = jnp.concatenate([weighted[slot, :, c * CHUNK:(c + 1) * CHUNK] for c in range(B // SIDE)])
+        every = dot(every, apart)
         for c in range(B // SIDE):
-            here = dot(weighted[slot, :, c * CHUNK:(c + 1) * CHUNK], apart)
+            here = every[c * B:(c + 1) * B]
             moment[slot, c] = here
             row = sum(jnp.where(lane == n, ir[c * SIDE + n:c * SIDE + n + 1], 0.0) for n in range(SIDE))
             rhs_add += here * row
@@ -193,16 +196,15 @@
 def item_kernel(places, turned, moment, users, wpairs, table, out, gram, rhs):
     gram[...] = jnp.zeros_like(gram)
     rhs[...] = jnp.zeros_like(rhs)
-    one, two, put = table[:R], table[R:2 * R], table[2 * R:]
+    one, two, put = table[:R], table[R:2 * R], table[2 * R:TABLE.shape[0]]
 
     def block(slot):
         ubase = pl.multiple_of(places[slot, 0] * B, B)
         ibase = pl.multiple_of(places[slot, 1] * B, B)
-        rows = users[pl.ds(ubase, B), :][:, :R]
-        parts = three(rows, 1)
-        upairs = dot(parts, jnp.concatenate([one] * PACK)) * dot(parts, jnp.concatenate([two] * PACK))
+        rows = users[pl.ds(ubase, B), :]
+        upairs = dot(rows, jnp.concatenate([one] * PACK)) * dot(rows, jnp.concatenate([two] * PACK))
         gram[pl.ds(ibase, B), :] += paired(turned, slot, upairs, wpairs[slot].reshape(B // 16, 16, WIDTH))
-        urows = jnp.concatenate([rows] * PACK, axis=1)
+        urows = dot(rows, fold())
         sums = three(jnp.sum(moment[slot] * urows[None], axis=1), 0)
         spread = iota((B, B), 1) % (B // SIDE) == item_at((B, B), 0) // SIDE
         sums = dot(jnp.where(spread, 1.0, 0.0).astype(bf16), sums)
@@ -275,7 +277,11 @@
     answer = jnp.concatenate(answer + [jnp.zeros((LANES - R, LANES), f32)], axis=0)
     answer = jnp.transpose(answer)[:T]
     out[...] = answer[:, :R]
-    copies[...] = jnp.broadcast_to(answer[None], copies.shape)
+    if copies.dtype == bf16:
+        answer = three(answer[:, :R], 1).astype(f32)
+        copies[...] = jnp.concatenate([answer] * (copies.shape[0] // T)).astype(bf16)
+    else:
+        copies[...] = jnp.broadcast_to(answer[None], copies.shape)
 
 
 def vmem():
@@ -304,13 +310,12 @@
             pltpu.VMEM(values.shape, bf16),
             pltpu.VMEM(values.shape, bf16),
             pltpu.VMEM(values.shape, bf16),
-            pltpu.VMEM((IBD * B, WIDTH), f32),
             pltpu.VMEM((IBD * B, LANES), f32),
-            pltpu.VMEM(table.shape, bf16),
+            pltpu.VMEM((table.shape[0] + IBD * B, WIDTH), bf16),
             jax.ShapeDtypeStruct((2, 4), jnp.int32),
         ),
         in_specs=[anywhere(), smem()] + [anywhere()] * 4,
-        out_specs=[vmem()] * 6 + [smem()],
+        out_specs=[vmem()] * 5 + [smem()],
         scratch_shapes=[
             pltpu.SMEM(coords.shape, jnp.int32), pltpu.VMEM(values.shape, bf16), pltpu.VMEM(observed.shape, jnp.int32), pltpu.VMEM(items.shape, f32),
             pltpu.VMEM((B * B // 2, LANES), f32), pltpu.SemaphoreType.DMA((7,)),
@@ -319,7 +324,7 @@
     )(coords, counts, values, observed, items, table)
 
 
-def user_equations(places, weeks, mask, weighted, ipairs, irows, table):
+def user_equations(places, weeks, mask, weighted, irows, table):
     return pl.pallas_call(
         user_kernel,
         out_shape=(
@@ -327,11 +332,11 @@
             pltpu.VMEM((2, B, WIDTH), bf16),
             pltpu.VMEM((2, B // SIDE, B, LANES), f32),
         ),
-        in_specs=[smem()] + [vmem()] * 6,
+        in_specs=[smem()] + [vmem()] * 5,
         out_specs=[vmem()] * 3,
         scratch_shapes=[pltpu.VMEM((UBD * B, WIDTH), f32), pltpu.VMEM((UBD * B, R), f32)],
         compiler_params=params(16),
-    )(places, weeks, mask, weighted, ipairs, irows, table)
+    )(places, weeks, mask, weighted, irows, table)
 
 
 def item_equations(places, turned, moment, users, wpairs, table):
@@ -345,10 +350,10 @@
     )(places, turned, moment, users, wpairs, table)
 
 
-def solve(parts, peers):
+def solve(parts, copies):
     return pl.pallas_call(
         solve_kernel,
-        out_shape=(jax.ShapeDtypeStruct((T, R), f32), pltpu.VMEM((peers, T, LANES), f32)),
+        out_shape=(jax.ShapeDtypeStruct((T, R), f32), copies),
         in_specs=[vmem()],
         out_specs=(vmem(), vmem()),
         compiler_params=params(16),
@@ -397,14 +402,14 @@
     pair = lax.all_gather(week_factors, "core", axis=0, tiled=True)
     copies = week_copies(pair, n_slab * n_fib // 2)
     weeks = exchange(copies, ("z", "x", "y"))
-    mask, turned, weighted, ipairs, irows, table, places = prepare(
+    mask, turned, weighted, irows, table, places = prepare(
         coords[0], counts, values[0], observed[0], item_factors.T, jnp.asarray(TABLE, bf16)
     )
-    parts, wpairs, moment = user_equations(places, weeks, mask, weighted, ipairs, irows, table)
-    user_out, copies = solve(exchange(parts, FIBS), n_fib)
-    users = exchange(copies, FIBS).reshape(UBD * B, LANES)
+    parts, wpairs, moment = user_equations(places, weeks, mask, weighted, irows, table)
+    user_out, copies = solve(exchange(parts, FIBS), pltpu.VMEM((n_fib * T, LANES), bf16))
+    users = exchange(copies, FIBS)
     parts = item_equations(places, turned, moment, users, wpairs, table)
-    _, copies = solve(exchange(parts, SLABS), n_slab)
+    _, copies = solve(exchange(parts, SLABS), pltpu.VMEM((n_slab, T, LANES), f32))
     item_updated = exchange(copies, SLABS).reshape(IBD * B, LANES)[:, :R]
     return (user_out, item_updated)
 

time: 108 us -> 107 us (level)
  local copies, waits for them, and re-layouts: 2.37 us -> 0.68 us
  starting transfers between devices: 17 us -> 18.1 us
    unnamed x5 -> x1, local copies, waits for them, and re-layouts: 2.37 us -> 0.68 us
where the time goes in v4:
time: 107 us; the launch traced here: 106 us
  blocking collectives  66.6 us (62%)
  starting transfers between devices  18.1 us (17%)
  Pallas kernels  12.6 us (12%)
  waiting for transfers between devices  7.18 us (7%)
  between operations  1.31 us (1%)
    all_to_all x4, blocking collectives, exchange(): return lax.all_to_all(x, axis, 0, 0, tiled=True)  58.1 us
    all_to_all x1, starting transfers between devices, exchange(): return lax.all_to_all(x, axis, 0, 0, tiled=True)  18.1 us
    all_gather x1, blocking collectives, shards(): pair = lax.all_gather(week_factors, 'core', axis=0, tiled=True)  8.49 us
    all_to_all x1, waiting for transfers between devices, exchange(): return lax.all_to_all(x, axis, 0, 0, tiled=True)  7.18 us
    pallas_call x1, Pallas kernels, prepare(): pl.pallas_call(prepare_kernel, out_shape=(pltpu.VMEM(values.shape, bf16),...  4.07 us
    pallas_call x2, Pallas kernels, solve(): pl.pallas_call(solve_kernel, out_shape=(jax.ShapeDtypeStruct((T, R), f32)...  2.85 us
    pallas_call x1, Pallas kernels, user_equations(): pl.pallas_call(user_kernel, out_shape=(pltpu.VMEM((UBD * B, WIDTH), LINK)...  2.63 us
    pallas_call x1, Pallas kernels, item_equations(): pl.pallas_call(item_kernel, out_shape=pltpu.VMEM((IBD * B, WIDTH), LINK),...  2.31 us
  transfers between devices with their start and end apart: 1, of which 1 were waited for; matrix products, arithmetic and copies ran while one was open for 0% of the time, Pallas kernels for 4%

profile of v4, /device:TPU:1, one launch (start us, length us, event | category | flops | bytes accessed | tf_op | source)
XLA Modules:
  0.0 106.5 jit_solution(6258779013047821133)
XLA Ops:
  0.6 8.5 %all-gather = f32[2,4,32]{2,1,0:T(4,128)S(1)} all-gather(f32[1,4,32]{2,1,0:T(4,128)} %bitcast.25), channel_id=1, replica_groups=mesh['z'=8,'core'=2,'x'=4,'y'=8] {'core'}, dimensions={0}, use_global_device_ids=true | all-gather | bytes 1536 | tf_op jit(solution)/shard_map/all_gather | solution.py:402
  9.1 0.8 shard_map.87
  9.9 18.1 %all-to-all-start = ((bf16[256,2,128]{2,1,0:T(2,128)(2,1)}), bf16[256,2,128]{2,1,0:T(2,128)(2,1)}, u32[]{:S(2)}, u32[]{:S(2)}) async-start(bf16[256,2,128]{2,1,0:T(2,128)(2,1)} %shard_map.87), calls=%async_computation | async-start | bytes 262144 | tf_op jit(solution)/shard_map/all_to_all | solution.py:397
  28.6 4.1 %shard_map.86 = (bf16[2,64,4096]{2,1,0:T(8,128)(2,1)S(1)}, bf16[2,64,4096]{2,1,0:T(8,128)(2,1)S(1)}, bf16[2,64,4096]{2,1,0:T(8,128)(2,1)S(1)}, f32[128,128]{1,0:...) custom-call(s32[2,3]{1,0:T(2,128)} %bitcast.26, s32[1,1]{1,0:T(1,128)S(6)} %copy.12.counts, ...), custom_call_target="tpu_custom_call" | custom-call | tf_op jit(solution)/shard_map/pallas_call | solution.py:307
  32.7 7.2 %all-to-all-done.weeks = bf16[256,2,128]{2,1,0:T(2,128)(2,1)} async-done(((bf16[256,2,128]{2,1,0:T(2,128)(2,1)}), bf16[256,2,128]{2,1,0:T(2,128)(2,1)}, u32[]{:S(2)}, u32[]{:S(2)}) %all-to-all-start) | async-done | bytes 131104 | tf_op jit(solution)/shard_map/all_to_all | solution.py:397
  39.9 2.6 %shard_map.88 = (bf16[256,640]{1,0:T(8,128)(2,1)S(1)}, bf16[2,64,640]{2,1,0:T(8,128)(2,1)S(1)}, f32[2,16,64,128]{3,2,1,0:T(8,128)S(1)}) custom-call(s32[2,4]{1,0:T(2,128)S(1)} %get-tuple-element.14.places, bf16[256,2,128]{2,1,0:T(2,128)(2,1)} %all-to-all-done.weeks, bf16[2,64,4096]{2,1,0:T(8,128)(2,1)S(1)} %get-tuple-element.15.mask, ...), custom_call_target="tpu_custom_call" | custom-call | tf_op jit(solution)/shard_map/pallas_call | solution.py:328
  42.5 14.4 %all_to_all.43 = bf16[32,8,640]{2,1,0:T(8,128)(2,1)S(1)} all-to-all(bf16[32,8,640]{2,1,0:T(8,128)(2,1)S(1)} %bitcast.17), channel_id=1, replica_groups=mesh['z'=8,'core'=2,'x'=4,'y'=8] {'x','y'}, dimensions={0} | all-to-all | bytes 655360 | tf_op jit(solution)/shard_map/all_to_all | solution.py:397
  56.9 1.4 %shard_map.89 = (f32[8,32]{1,0:T(8,128)}, bf16[256,128]{1,0:T(8,128)(2,1)S(1)}) custom-call(bf16[256,640]{1,0:T(8,128)(2,1)S(1)} %bitcast.14), custom_call_target="tpu_custom_call" | custom-call | tf_op jit(solution)/shard_map/pallas_call | solution.py:354
  58.4 14.7 %all_to_all.44 = bf16[32,8,128]{2,1,0:T(8,128)(2,1)S(1)} all-to-all(bf16[32,8,128]{2,1,0:T(8,128)(2,1)S(1)} %bitcast.19), channel_id=1, replica_groups=mesh['z'=8,'core'=2,'x'=4,'y'=8] {'x','y'}, dimensions={0} | all-to-all | bytes 131072 | tf_op jit(solution)/shard_map/all_to_all | solution.py:397
  73.1 2.3 %shard_map.90 = bf16[128,640]{1,0:T(8,128)(2,1)S(1)} custom-call(s32[2,4]{1,0:T(2,128)S(1)} %get-tuple-element.14.places, bf16[2,64,4096]{2,1,0:T(8,128)(2,1)S(1)} %get-tuple-element.21.turned, f32[2,16,64,128]{3,2,1,0:T(8,128)S(1)} %get-tuple-element.22.moment, bf16[256,128]{1,0:T(8,128)(2,1)S(1)} %bitcast.18, ...), custom_call_target="tpu_custom_call" | custom-call | tf_op jit(solution)/shard_map/pallas_call | solution.py:343
  75.4 18.5 %all_to_all.45 = bf16[16,8,640]{2,1,0:T(8,128)(2,1)S(1)} all-to-all(bf16[16,8,640]{2,1,0:T(8,128)(2,1)S(1)} %bitcast.15), channel_id=1, replica_groups=mesh['z'=8,'core'=2,'x'=4,'y'=8] {'z','core'}, dimensions={0} | all-to-all | bytes 327680 | tf_op jit(solution)/shard_map/all_to_all | solution.py:397
  93.9 1.4 %shard_map.91 = (f32[8,32]{1,0:T(8,128)}, f32[16,8,128]{2,1,0:T(8,128)S(1)}) custom-call(bf16[128,640]{1,0:T(8,128)(2,1)S(1)} %bitcast.16), custom_call_target="tpu_custom_call" | custom-call | tf_op jit(solution)/shard_map/pallas_call | solution.py:354
  95.3 10.4 %all_to_all.46 = f32[16,8,128]{2,1,0:T(8,128)S(1)} all-to-all(f32[16,8,128]{2,1,0:T(8,128)S(1)} %get-tuple-element.25), channel_id=1, replica_groups=mesh['z'=8,'core'=2,'x'=4,'y'=8] {'z','core'}, dimensions={0} | all-to-all | bytes 131072 | tf_op jit(solution)/shard_map/all_to_all | solution.py:397
  105.8 0.7 copy.11
Async XLA Ops:
  9.9 30.0 %all-to-all-start = ((bf16[256,2,128]{2,1,0:T(2,128)(2,1)}), bf16[256,2,128]{2,1,0:T(2,128)(2,1)}, u32[]{:S(2)}, u32[]{:S(2)}) async-start(bf16[256,2,128]{2,1,0:T(2,128)(2,1)} %shard_map.87), calls=%async_computation | async-start | bytes 262144 | tf_op jit(solution)/shard_map/all_to_all | solution.py:397

commit v5 on v4

--- a/solution.py
+++ b/solution.py
@@ -67,16 +67,24 @@
     return lax.broadcasted_iota(jnp.int32, shape, dim)
 
 
-def week_block(weeks, one, two, start):
-    slab, part = start // (FIB // WROWS), start % (FIB // WROWS)
-    both = weeks[pl.ds(slab // 2 * FIB + part * WROWS, WROWS)].astype(f32)
-    packed = jnp.where(slab % 2 == 0, both[:, 0], both[:, 1]).astype(bf16)
-    spread = (iota((B, WROWS), 0) // PACK == iota((B, WROWS), 1)).astype(f32).astype(bf16)
+def week_blocks(weeks, one, two, starts):
+    packed = []
+    for start in starts:
+        slab, part = start // (FIB // WROWS), start % (FIB // WROWS)
+        both = weeks[pl.ds(slab // 2 * FIB + part * WROWS, WROWS)].astype(f32)
+        packed.append(jnp.where(slab % 2 == 0, both[:, 0], both[:, 1]))
+    packed = jnp.concatenate(packed).astype(bf16)
+    count = len(starts) * B
+    spread = (iota((count, count // PACK), 0) // PACK == iota((count, count // PACK), 1)).astype(f32).astype(bf16)
     rows = dot(spread, packed)
-    own = iota((B, LANES), 0) % PACK == iota((B, LANES), 1) // R
+    own = iota(rows.shape, 0) % PACK == iota(rows.shape, 1) // R
     rows = jnp.where(own, rows, 0.0).astype(bf16)
     pairs = dot(rows, jnp.concatenate([one] * PACK)) * dot(rows, jnp.concatenate([two] * PACK))
-    return pairs.astype(bf16), dot(rows, fold()).astype(bf16)
+    return pairs.astype(bf16), dot(rows, fold())
+
+
+def together(first, second, same):
+    return first + jnp.where(same, second, 0.0), second + jnp.where(same, first, 0.0)
 
 
 def unfold(x):
@@ -100,21 +108,28 @@
     return (gram + dot(parts, put)).astype(LINK)
 
 
-def turn(own, strips, turned, slot):
+def turn(own, strips):
     pairs = B // 2
     for t in range(pairs):
         strips[t * B:(t + 1) * B] = own[:, t * LANES:(t + 1) * LANES]
     first = iota((pairs, LANES), 1) < B
+    tiles = []
     for v in range(pairs):
         a, b = (strips[pl.ds(2 * v + n, pairs, stride=B)] for n in range(2))
         even = jnp.where(first, a, pltpu.roll(b, B, 1))
         odd = jnp.where(first, pltpu.roll(a, B, 1), b)
-        turned[slot, :, v * LANES:(v + 1) * LANES] = jnp.concatenate([even, odd]).astype(bf16)
-
-
-def item_at(rows, dim):
-    place = iota(rows, dim) % B
-    return iota(rows, dim) // B * B + place % (B // 2) * 2 + place // (B // 2)
+        tiles.append(jnp.concatenate([even, odd]).astype(bf16))
+    place = iota((B, B), 1)
+    order = place % pairs * 2 + place // pairs == iota((B, B), 0)
+    return dot(jnp.where(order, 1.0, 0.0).astype(bf16), jnp.concatenate(tiles, axis=1)).astype(bf16)
+
+
+def four_a_row(rows):
+    count = rows.shape[0]
+    own = iota(rows.shape, 0) % PACK == iota(rows.shape, 1) // R
+    parts = three(jnp.where(own, rows, 0.0), 0)
+    pick = iota((count // PACK, 4 * count), 1) % count // PACK == iota((count // PACK, 4 * count), 0)
+    return dot(jnp.where(pick, 1.0, 0.0).astype(bf16), parts)
 
 
 def paired(mask, slot, pairs, wp):
@@ -125,7 +140,7 @@
         for i in range(c, c + step):
             row = jnp.broadcast_to(pairs[i:i + 1], (16, WIDTH)).astype(bf16)
             outer.append((wp * row[None]).reshape(B, WIDTH))
-        total += dot(mask[slot, :, c * B:(c + step) * B], jnp.concatenate(outer))
+        total += dot(mask[slot, :, c * B:(c + step) * B].astype(bf16), jnp.concatenate(outer))
     return total
 
 
@@ -144,82 +159,74 @@
     pairs = dot(rows, jnp.concatenate([table[:R]] * PACK), (0, 0))
     pairs *= dot(rows, jnp.concatenate([table[R:2 * R]] * PACK), (0, 0))
     table[TABLE.shape[0]:] = pairs.astype(bf16)
-    irows[...] = dot(rows, fold(), (0, 0))
+    irows[...] = four_a_row(dot(rows, fold(), (0, 0)))
     for slot in range(2):
         moves[2 + 2 * slot].wait()
         moves[3 + 2 * slot].wait()
         own = observed[slot].astype(f32)
-        mask[slot] = own.astype(bf16)
+        if slot > 0:
+            own = jnp.where(counts[0, 0] > slot, own, 0.0)
+        mask[slot] = own.astype(bf16).astype(jnp.float8_e4m3fn)
         weighted[slot] = (values[slot].astype(f32) * own).astype(bf16)
-        turn(own, strips, turned, slot)
+        turned[slot] = turn(own, strips).astype(turned.dtype)
     moves[6].wait()
     for slot in range(2):
         for n in range(3):
             places[slot, n] = coords[slot, n]
-        places[slot, 3] = counts[0, 0]
-
-
-def user_kernel(places, weeks, mask, weighted, irows, table, out, wpairs, moment, gram, rhs):
-    gram[...] = jnp.zeros_like(gram)
-    rhs[...] = jnp.zeros_like(rhs)
+
+
+def user_kernel(places, weeks, mask, weighted, irows, table, out, wpairs, moment):
     one, two, put = table[:R], table[R:2 * R], table[2 * R:TABLE.shape[0]]
-
-    def block(slot):
-        ubase = pl.multiple_of(places[slot, 0] * B, B)
+    pairs, rows = week_blocks(weeks, one, two, [places[slot, 2] for slot in range(2)])
+    out[...] = jnp.zeros_like(out)
+    apart = iota((CHUNK, LANES), 0) // B == iota((CHUNK, LANES), 1) // R
+    gram, rhs = [], []
+    for slot in range(2):
         ibase = pl.multiple_of(places[slot, 1] * B, B)
-        wp, wr = week_block(weeks, one, two, places[slot, 2])
+        wp, wr = pairs[slot * B:(slot + 1) * B], rows[slot * B:(slot + 1) * B]
         wpairs[slot] = wp
-        gram[pl.ds(ubase, B), :] += paired(mask, slot, table[pl.ds(pl.multiple_of(TABLE.shape[0] + ibase, B), B), :].astype(f32), wp.reshape(B // 16, 16, WIDTH))
-        ir = irows[pl.ds(ibase, B), :]
-        lane = iota((1, LANES), 1) // R
-        apart = iota((CHUNK, LANES), 0) // B == iota((CHUNK, LANES), 1) // R
-        apart = jnp.where(apart, jnp.concatenate([wr.astype(f32)] * SIDE), 0.0).astype(bf16)
-        rhs_add = jnp.zeros((B, LANES), f32)
+        ip = table[pl.ds(pl.multiple_of(TABLE.shape[0] + ibase, B), B), :].astype(f32)
+        ir = irows[pl.ds(pl.multiple_of(places[slot, 1] * (B // PACK), B // PACK), B // PACK), :]
         every = jnp.concatenate([weighted[slot, :, c * CHUNK:(c + 1) * CHUNK] for c in range(B // SIDE)])
-        every = dot(every, apart)
+        every = dot(every, jnp.where(apart, jnp.concatenate([wr] * SIDE), 0.0).astype(bf16))
+        total = jnp.zeros((B, LANES), f32)
         for c in range(B // SIDE):
             here = every[c * B:(c + 1) * B]
             moment[slot, c] = here
-            row = sum(jnp.where(lane == n, ir[c * SIDE + n:c * SIDE + n + 1], 0.0) for n in range(SIDE))
-            rhs_add += here * row
-        rhs[pl.ds(ubase, B), :] += unfold(rhs_add)
-
-    block(0)
-
-    @pl.when(places[0, 3] > 1)
-    def _():
-        block(1)
-
-    out[...] = send_form(gram[...], rhs[...], put)
-
-
-def item_kernel(places, turned, moment, users, wpairs, table, out, gram, rhs):
-    gram[...] = jnp.zeros_like(gram)
-    rhs[...] = jnp.zeros_like(rhs)
+            total += here * ir[c:c + 1]
+        rhs.append(total)
+        gram.append(paired(mask, slot, ip, wp.reshape(B // 16, 16, WIDTH)))
+    same = places[0, 0] == places[1, 0]
+    rhs = unfold(jnp.concatenate(together(*rhs, same)))
+    sent = send_form(jnp.concatenate(together(*gram, same)), rhs, put)
+    for slot in range(2):
+        out[pl.ds(pl.multiple_of(places[slot, 0] * B, B), B), :] = sent[slot * B:(slot + 1) * B]
+
+
+def item_kernel(places, turned, moment, users, wpairs, table, out):
     one, two, put = table[:R], table[R:2 * R], table[2 * R:TABLE.shape[0]]
-
-    def block(slot):
-        ubase = pl.multiple_of(places[slot, 0] * B, B)
-        ibase = pl.multiple_of(places[slot, 1] * B, B)
-        rows = users[pl.ds(ubase, B), :]
-        upairs = dot(rows, jnp.concatenate([one] * PACK)) * dot(rows, jnp.concatenate([two] * PACK))
-        gram[pl.ds(ibase, B), :] += paired(turned, slot, upairs, wpairs[slot].reshape(B // 16, 16, WIDTH))
-        urows = dot(rows, fold())
-        sums = three(jnp.sum(moment[slot] * urows[None], axis=1), 0)
-        spread = iota((B, B), 1) % (B // SIDE) == item_at((B, B), 0) // SIDE
-        sums = dot(jnp.where(spread, 1.0, 0.0).astype(bf16), sums)
-        sums = jnp.where(item_at(sums.shape, 0) % SIDE == iota(sums.shape, 1) // R, sums, 0.0)
-        rhs[pl.ds(ibase, B), :] += unfold(sums)
-
-    block(0)
-
-    @pl.when(places[0, 3] > 1)
-    def _():
-        block(1)
-
-    count = IBD * B
-    order = jnp.where(item_at((count, count), 1) == iota((count, count), 0), 1.0, 0.0).astype(bf16)
-    out[...] = dot(order, send_form(gram[...], rhs[...], put)).astype(LINK)
+    rows = jnp.concatenate([users[pl.ds(pl.multiple_of(places[slot, 0] * B, B), B), :] for slot in range(2)])
+    pairs = dot(rows, jnp.concatenate([one] * PACK)) * dot(rows, jnp.concatenate([two] * PACK))
+    rows = dot(rows, fold())
+    out[...] = jnp.zeros_like(out)
+    gram, sums = [], []
+    for slot in range(2):
+        here = slice(slot * B, (slot + 1) * B)
+        gram.append(paired(turned, slot, pairs[here], wpairs[slot].reshape(B // 16, 16, WIDTH)))
+        sums.append(jnp.sum(moment[slot] * rows[here][None], axis=1))
+    parts = three(jnp.concatenate(sums), 0)
+    count = 2 * B
+    spread = iota((count, count), 1) % (count // PACK) == iota((count, count), 0) // PACK
+    rhs = dot(jnp.where(spread, 1.0, 0.0).astype(bf16), parts)
+    rhs = jnp.where(iota(rhs.shape, 0) % PACK == iota(rhs.shape, 1) // R, rhs, 0.0)
+    same = places[0, 1] == places[1, 1]
+    rhs = jnp.concatenate(together(rhs[:B], rhs[B:], same))
+    high = rhs.astype(bf16).astype(f32)
+    parts = jnp.concatenate([high, rhs - high], axis=1).astype(bf16)
+    wide = jnp.concatenate([put[:R]] * PACK + [put[R:]] * PACK)
+    sent = (jnp.concatenate(together(*gram, same)) + dot(parts, wide)).astype(LINK)
+    for slot in range(2):
+        out[pl.ds(pl.multiple_of(places[slot, 1] * B, B), B), :] = sent[slot * B:(slot + 1) * B]
 
 
 def solve_kernel(parts, out, copies):
@@ -307,12 +314,12 @@
     return pl.pallas_call(
         prepare_kernel,
         out_shape=(
+            pltpu.VMEM(values.shape, jnp.float8_e4m3fn),
+            pltpu.VMEM(values.shape, jnp.float8_e4m3fn),
             pltpu.VMEM(values.shape, bf16),
-            pltpu.VMEM(values.shape, bf16),
-            pltpu.VMEM(values.shape, bf16),
-            pltpu.VMEM((IBD * B, LANES), f32),
+            pltpu.VMEM((IBD * B // PACK, LANES), f32),
             pltpu.VMEM((table.shape[0] + IBD * B, WIDTH), bf16),
-            jax.ShapeDtypeStruct((2, 4), jnp.int32),
+            jax.ShapeDtypeStruct((2, 3), jnp.int32),
         ),
         in_specs=[anywhere(), smem()] + [anywhere()] * 4,
         out_specs=[vmem()] * 5 + [smem()],
@@ -334,7 +341,6 @@
         ),
         in_specs=[smem()] + [vmem()] * 5,
         out_specs=[vmem()] * 3,
-        scratch_shapes=[pltpu.VMEM((UBD * B, WIDTH), f32), pltpu.VMEM((UBD * B, R), f32)],
         compiler_params=params(16),
     )(places, weeks, mask, weighted, irows, table)
 
@@ -345,7 +351,6 @@
         out_shape=pltpu.VMEM((IBD * B, WIDTH), LINK),
         in_specs=[smem()] + [vmem()] * 5,
         out_specs=vmem(),
-        scratch_shapes=[pltpu.VMEM((IBD * B, WIDTH), f32), pltpu.VMEM((IBD * B, R), f32)],
         compiler_params=params(16),
     )(places, turned, moment, users, wpairs, table)
 

time: 107 us -> 105 us (0.981)
  blocking collectives: 66.6 us -> 65.2 us
  starting transfers between devices: 18.1 us -> 17 us
  Pallas kernels: 12.6 us -> 13.7 us
    all_to_all x4, blocking collectives: 58.1 us -> 56.7 us  [exchange(): return lax.all_to_all(x, axis, 0, 0, tiled=True)]
    all_to_all x1, starting transfers between devices: 18.1 us -> 17 us  [exchange(): return lax.all_to_all(x, axis, 0, 0, tiled=True)]
where the time goes in v5:
time: 105 us
  blocking collectives  65.2 us (62%)
  starting transfers between devices  17 us (16%)
  Pallas kernels  13.7 us (13%)
  waiting for transfers between devices  7.24 us (7%)
  between operations  1.31 us (1%)
    all_to_all x4, blocking collectives, exchange(): return lax.all_to_all(x, axis, 0, 0, tiled=True)  56.7 us
    all_to_all x1, starting transfers between devices, exchange(): return lax.all_to_all(x, axis, 0, 0, tiled=True)  17 us
    all_gather x1, blocking collectives, shards(): pair = lax.all_gather(week_factors, 'core', axis=0, tiled=True)  8.49 us
    all_to_all x1, waiting for transfers between devices, exchange(): return lax.all_to_all(x, axis, 0, 0, tiled=True)  7.24 us
    pallas_call x1, Pallas kernels, prepare(): pl.pallas_call(prepare_kernel, out_shape=(pltpu.VMEM(values.shape, jnp.fl...  4.39 us
    pallas_call x1, Pallas kernels, user_equations(): pl.pallas_call(user_kernel, out_shape=(pltpu.VMEM((UBD * B, WIDTH), LINK)...  2.92 us
    pallas_call x2, Pallas kernels, solve(): pl.pallas_call(solve_kernel, out_shape=(jax.ShapeDtypeStruct((T, R), f32)...  2.85 us
    pallas_call x1, Pallas kernels, item_equations(): pl.pallas_call(item_kernel, out_shape=pltpu.VMEM((IBD * B, WIDTH), LINK),...  2.71 us
  transfers between devices with their start and end apart: 1, of which 1 were waited for; matrix products, arithmetic and copies ran while one was open for 0% of the time, Pallas kernels for 4%

profile of v5, /device:TPU:1, one launch (start us, length us, event | category | flops | bytes accessed | tf_op | source)
XLA Modules:
  0.0 105.1 jit_solution(8410688938665337084)
XLA Ops:
  0.6 8.5 %all-gather = f32[2,4,32]{2,1,0:T(4,128)S(1)} all-gather(f32[1,4,32]{2,1,0:T(4,128)} %bitcast.25), channel_id=1, replica_groups=mesh['z'=8,'core'=2,'x'=4,'y'=8] {'core'}, dimensions={0}, use_global_device_ids=true | all-gather | bytes 1536 | tf_op jit(solution)/shard_map/all_gather | solution.py:407
  9.1 0.8 shard_map.87
  9.9 17.0 %all-to-all-start = ((bf16[256,2,128]{2,1,0:T(2,128)(2,1)}), bf16[256,2,128]{2,1,0:T(2,128)(2,1)S(1)}, u32[]{:S(2)}, u32[]{:S(2)}) async-start(bf16[256,2,128]{2,1,0:T(2,128)(2,1)} %shard_map.87), calls=%async_computation | async-start | bytes 262144 | tf_op jit(solution)/shard_map/all_to_all | solution.py:402
  27.6 4.4 %shard_map.86 = (f8e4m3fn[2,64,4096]{2,1,0:T(32,128)(4,1)S(1)}, f8e4m3fn[2,64,4096]{2,1,0:T(32,128)(4,1)S(1)}, bf16[2,64,4096]{2,1,0:T(8,128)(2,1)S(1)}, f32[32,...) custom-call(s32[2,3]{1,0:T(2,128)} %bitcast.26, s32[1,1]{1,0:T(1,128)S(6)} %copy.12.counts, ...), custom_call_target="tpu_custom_call" | custom-call | tf_op jit(solution)/shard_map/pallas_call | solution.py:314
  32.0 7.2 %all-to-all-done.weeks = bf16[256,2,128]{2,1,0:T(2,128)(2,1)S(1)} async-done(((bf16[256,2,128]{2,1,0:T(2,128)(2,1)}), bf16[256,2,128]{2,1,0:T(2,128)(2,1)S(1)}, u32[]{:S(2)}, u32[]{:S(2)}) %all-to-all-start) | async-done | bytes 131104 | tf_op jit(solution)/shard_map/all_to_all | solution.py:402
  39.2 2.9 %shard_map.88 = (bf16[256,640]{1,0:T(8,128)(2,1)S(1)}, bf16[2,64,640]{2,1,0:T(8,128)(2,1)S(1)}, f32[2,16,64,128]{3,2,1,0:T(8,128)S(1)}) custom-call(s32[2,3]{1,0:T(2,128)S(1)} %get-tuple-element.14.places, bf16[256,2,128]{2,1,0:T(2,128)(2,1)S(1)} %all-to-all-done.weeks, f8e4m3fn[2,64,4096]{2,1,0:T(32,128)(4,1)S(1)} %get-tuple-element.15.mask, ...), custom_call_target="tpu_custom_call" | custom-call | tf_op jit(solution)/shard_map/pallas_call | solution.py:335
  42.1 13.4 %all_to_all.43 = bf16[32,8,640]{2,1,0:T(8,128)(2,1)S(1)} all-to-all(bf16[32,8,640]{2,1,0:T(8,128)(2,1)S(1)} %bitcast.17), channel_id=1, replica_groups=mesh['z'=8,'core'=2,'x'=4,'y'=8] {'x','y'}, dimensions={0} | all-to-all | bytes 655360 | tf_op jit(solution)/shard_map/all_to_all | solution.py:402
  55.5 1.4 %shard_map.89 = (f32[8,32]{1,0:T(8,128)}, bf16[256,128]{1,0:T(8,128)(2,1)S(1)}) custom-call(bf16[256,640]{1,0:T(8,128)(2,1)S(1)} %bitcast.14), custom_call_target="tpu_custom_call" | custom-call | tf_op jit(solution)/shard_map/pallas_call | solution.py:359
  56.9 15.6 %all_to_all.44 = bf16[32,8,128]{2,1,0:T(8,128)(2,1)S(1)} all-to-all(bf16[32,8,128]{2,1,0:T(8,128)(2,1)S(1)} %bitcast.19), channel_id=1, replica_groups=mesh['z'=8,'core'=2,'x'=4,'y'=8] {'x','y'}, dimensions={0} | all-to-all | bytes 131072 | tf_op jit(solution)/shard_map/all_to_all | solution.py:402
  72.5 2.7 %shard_map.90 = bf16[128,640]{1,0:T(8,128)(2,1)S(1)} custom-call(s32[2,3]{1,0:T(2,128)S(1)} %get-tuple-element.14.places, f8e4m3fn[2,64,4096]{2,1,0:T(32,128)(4,1)S(1)} %get-tuple-element.21.turned, f32[2,16,64,128]{3,2,1,0:T(8,128)S(1)} %get-tuple-element.22.moment, bf16[256,128]{1,0:T(8,128)(2,1)S(1)} %bitcast.18, ...), custom_call_target="tpu_custom_call" | custom-call | tf_op jit(solution)/shard_map/pallas_call | solution.py:349
  75.2 17.3 %all_to_all.45 = bf16[16,8,640]{2,1,0:T(8,128)(2,1)S(1)} all-to-all(bf16[16,8,640]{2,1,0:T(8,128)(2,1)S(1)} %bitcast.15), channel_id=1, replica_groups=mesh['z'=8,'core'=2,'x'=4,'y'=8] {'z','core'}, dimensions={0} | all-to-all | bytes 327680 | tf_op jit(solution)/shard_map/all_to_all | solution.py:402
  92.5 1.4 %shard_map.91 = (f32[8,32]{1,0:T(8,128)}, f32[16,8,128]{2,1,0:T(8,128)S(1)}) custom-call(bf16[128,640]{1,0:T(8,128)(2,1)S(1)} %bitcast.16), custom_call_target="tpu_custom_call" | custom-call | tf_op jit(solution)/shard_map/pallas_call | solution.py:359
  93.9 10.4 %all_to_all.46 = f32[16,8,128]{2,1,0:T(8,128)S(1)} all-to-all(f32[16,8,128]{2,1,0:T(8,128)S(1)} %get-tuple-element.25), channel_id=1, replica_groups=mesh['z'=8,'core'=2,'x'=4,'y'=8] {'z','core'}, dimensions={0} | all-to-all | bytes 131072 | tf_op jit(solution)/shard_map/all_to_all | solution.py:402
  104.4 0.7 copy.11
Async XLA Ops:
  9.9 29.3 %all-to-all-start = ((bf16[256,2,128]{2,1,0:T(2,128)(2,1)}), bf16[256,2,128]{2,1,0:T(2,128)(2,1)S(1)}, u32[]{:S(2)}, u32[]{:S(2)}) async-start(bf16[256,2,128]{2,1,0:T(2,128)(2,1)} %shard_map.87), calls=%async_computation | async-start | bytes 262144 | tf_op jit(solution)/shard_map/all_to_all | solution.py:402

commit v6 on v5

--- a/solution.py
+++ b/solution.py
@@ -325,7 +325,7 @@
         out_specs=[vmem()] * 5 + [smem()],
         scratch_shapes=[
             pltpu.SMEM(coords.shape, jnp.int32), pltpu.VMEM(values.shape, bf16), pltpu.VMEM(observed.shape, jnp.int32), pltpu.VMEM(items.shape, f32),
-            pltpu.VMEM((B * B // 2, LANES), f32), pltpu.SemaphoreType.DMA((7,)),
+            pltpu.VMEM((B * B // 2 + B, LANES), f32), pltpu.SemaphoreType.DMA((7,)),
         ],
         compiler_params=params(16),
     )(coords, counts, values, observed, items, table)

time: 105 us -> 105 us (level)
  no operation moved by 1% of the time
where the time goes in v6:
time: 105 us
  blocking collectives  65.2 us (62%)
  starting transfers between devices  17 us (16%)
  Pallas kernels  13.7 us (13%)
  waiting for transfers between devices  7.24 us (7%)
  between operations  1.31 us (1%)
    all_to_all x4, blocking collectives, exchange(): return lax.all_to_all(x, axis, 0, 0, tiled=True)  56.7 us
    all_to_all x1, starting transfers between devices, exchange(): return lax.all_to_all(x, axis, 0, 0, tiled=True)  17 us
    all_gather x1, blocking collectives, shards(): pair = lax.all_gather(week_factors, 'core', axis=0, tiled=True)  8.49 us
    all_to_all x1, waiting for transfers between devices, exchange(): return lax.all_to_all(x, axis, 0, 0, tiled=True)  7.24 us
    pallas_call x1, Pallas kernels, prepare(): pl.pallas_call(prepare_kernel, out_shape=(pltpu.VMEM(values.shape, jnp.fl...  4.39 us
    pallas_call x1, Pallas kernels, user_equations(): pl.pallas_call(user_kernel, out_shape=(pltpu.VMEM((UBD * B, WIDTH), LINK)...  2.92 us
    pallas_call x2, Pallas kernels, solve(): pl.pallas_call(solve_kernel, out_shape=(jax.ShapeDtypeStruct((T, R), f32)...  2.85 us
    pallas_call x1, Pallas kernels, item_equations(): pl.pallas_call(item_kernel, out_shape=pltpu.VMEM((IBD * B, WIDTH), LINK),...  2.71 us
  transfers between devices with their start and end apart: 1, of which 1 were waited for; matrix products, arithmetic and copies ran while one was open for 0% of the time, Pallas kernels for 4%

profile of v6, /device:TPU:1, one launch (start us, length us, event | category | flops | bytes accessed | tf_op | source)
XLA Modules:
  0.0 105.1 jit_solution(11742534006394942389)
XLA Ops:
  0.6 8.5 %all-gather = f32[2,4,32]{2,1,0:T(4,128)S(1)} all-gather(f32[1,4,32]{2,1,0:T(4,128)} %bitcast.25), channel_id=1, replica_groups=mesh['z'=8,'core'=2,'x'=4,'y'=8] {'core'}, dimensions={0}, use_global_device_ids=true | all-gather | bytes 1536 | tf_op jit(solution)/shard_map/all_gather | solution.py:407
  9.1 0.8 shard_map.87
  9.9 17.0 %all-to-all-start = ((bf16[256,2,128]{2,1,0:T(2,128)(2,1)}), bf16[256,2,128]{2,1,0:T(2,128)(2,1)S(1)}, u32[]{:S(2)}, u32[]{:S(2)}) async-start(bf16[256,2,128]{2,1,0:T(2,128)(2,1)} %shard_map.87), calls=%async_computation | async-start | bytes 262144 | tf_op jit(solution)/shard_map/all_to_all | solution.py:402
  27.6 4.4 %shard_map.86 = (f8e4m3fn[2,64,4096]{2,1,0:T(32,128)(4,1)S(1)}, f8e4m3fn[2,64,4096]{2,1,0:T(32,128)(4,1)S(1)}, bf16[2,64,4096]{2,1,0:T(8,128)(2,1)S(1)}, f32[32,...) custom-call(s32[2,3]{1,0:T(2,128)} %bitcast.26, s32[1,1]{1,0:T(1,128)S(6)} %copy.12.counts, ...), custom_call_target="tpu_custom_call" | custom-call | tf_op jit(solution)/shard_map/pallas_call | solution.py:314
  32.0 7.2 %all-to-all-done.weeks = bf16[256,2,128]{2,1,0:T(2,128)(2,1)S(1)} async-done(((bf16[256,2,128]{2,1,0:T(2,128)(2,1)}), bf16[256,2,128]{2,1,0:T(2,128)(2,1)S(1)}, u32[]{:S(2)}, u32[]{:S(2)}) %all-to-all-start) | async-done | bytes 131104 | tf_op jit(solution)/shard_map/all_to_all | solution.py:402
  39.2 2.9 %shard_map.88 = (bf16[256,640]{1,0:T(8,128)(2,1)S(1)}, bf16[2,64,640]{2,1,0:T(8,128)(2,1)S(1)}, f32[2,16,64,128]{3,2,1,0:T(8,128)S(1)}) custom-call(s32[2,3]{1,0:T(2,128)S(1)} %get-tuple-element.14.places, bf16[256,2,128]{2,1,0:T(2,128)(2,1)S(1)} %all-to-all-done.weeks, f8e4m3fn[2,64,4096]{2,1,0:T(32,128)(4,1)S(1)} %get-tuple-element.15.mask, ...), custom_call_target="tpu_custom_call" | custom-call | tf_op jit(solution)/shard_map/pallas_call | solution.py:335
  42.1 13.4 %all_to_all.43 = bf16[32,8,640]{2,1,0:T(8,128)(2,1)S(1)} all-to-all(bf16[32,8,640]{2,1,0:T(8,128)(2,1)S(1)} %bitcast.17), channel_id=1, replica_groups=mesh['z'=8,'core'=2,'x'=4,'y'=8] {'x','y'}, dimensions={0} | all-to-all | bytes 655360 | tf_op jit(solution)/shard_map/all_to_all | solution.py:402
  55.5 1.4 %shard_map.89 = (f32[8,32]{1,0:T(8,128)}, bf16[256,128]{1,0:T(8,128)(2,1)S(1)}) custom-call(bf16[256,640]{1,0:T(8,128)(2,1)S(1)} %bitcast.14), custom_call_target="tpu_custom_call" | custom-call | tf_op jit(solution)/shard_map/pallas_call | solution.py:359
  56.9 15.6 %all_to_all.44 = bf16[32,8,128]{2,1,0:T(8,128)(2,1)S(1)} all-to-all(bf16[32,8,128]{2,1,0:T(8,128)(2,1)S(1)} %bitcast.19), channel_id=1, replica_groups=mesh['z'=8,'core'=2,'x'=4,'y'=8] {'x','y'}, dimensions={0} | all-to-all | bytes 131072 | tf_op jit(solution)/shard_map/all_to_all | solution.py:402
  72.5 2.7 %shard_map.90 = bf16[128,640]{1,0:T(8,128)(2,1)S(1)} custom-call(s32[2,3]{1,0:T(2,128)S(1)} %get-tuple-element.14.places, f8e4m3fn[2,64,4096]{2,1,0:T(32,128)(4,1)S(1)} %get-tuple-element.21.turned, f32[2,16,64,128]{3,2,1,0:T(8,128)S(1)} %get-tuple-element.22.moment, bf16[256,128]{1,0:T(8,128)(2,1)S(1)} %bitcast.18, ...), custom_call_target="tpu_custom_call" | custom-call | tf_op jit(solution)/shard_map/pallas_call | solution.py:349
  75.2 17.3 %all_to_all.45 = bf16[16,8,640]{2,1,0:T(8,128)(2,1)S(1)} all-to-all(bf16[16,8,640]{2,1,0:T(8,128)(2,1)S(1)} %bitcast.15), channel_id=1, replica_groups=mesh['z'=8,'core'=2,'x'=4,'y'=8] {'z','core'}, dimensions={0} | all-to-all | bytes 327680 | tf_op jit(solution)/shard_map/all_to_all | solution.py:402
  92.5 1.4 %shard_map.91 = (f32[8,32]{1,0:T(8,128)}, f32[16,8,128]{2,1,0:T(8,128)S(1)}) custom-call(bf16[128,640]{1,0:T(8,128)(2,1)S(1)} %bitcast.16), custom_call_target="tpu_custom_call" | custom-call | tf_op jit(solution)/shard_map/pallas_call | solution.py:359
  93.9 10.4 %all_to_all.46 = f32[16,8,128]{2,1,0:T(8,128)S(1)} all-to-all(f32[16,8,128]{2,1,0:T(8,128)S(1)} %get-tuple-element.25), channel_id=1, replica_groups=mesh['z'=8,'core'=2,'x'=4,'y'=8] {'z','core'}, dimensions={0} | all-to-all | bytes 131072 | tf_op jit(solution)/shard_map/all_to_all | solution.py:402
  104.4 0.7 copy.11
Async XLA Ops:
  9.9 29.3 %all-to-all-start = ((bf16[256,2,128]{2,1,0:T(2,128)(2,1)}), bf16[256,2,128]{2,1,0:T(2,128)(2,1)S(1)}, u32[]{:S(2)}, u32[]{:S(2)}) async-start(bf16[256,2,128]{2,1,0:T(2,128)(2,1)} %shard_map.87), calls=%async_computation | async-start | bytes 262144 | tf_op jit(solution)/shard_map/all_to_all | solution.py:402

commit v7 on v6

--- a/solution.py
+++ b/solution.py
@@ -263,13 +263,12 @@
     for k in range(R):
         own = k // T
         inverse = 1.0 / spread(rows[k, own], k % T)
-        scaled = {t: rows[k, t] * inverse for t in range(own, tiles)}
         mine = spread(side[own], k % T)
         right.append(mine * inverse)
         for t in range(own, tiles):
-            side[t] = side[t] - scaled[t] * mine
+            side[t] = side[t] - rows[k, t] * right[k]
         for r in range(k + 1, R):
-            factor[k, r] = spread(scaled[r // T], r % T)
+            factor[k, r] = spread(rows[k, r // T], r % T) * inverse
             for t in range(r // T, tiles):
                 rows[r, t] = rows[r, t] - factor[k, r] * rows[k, t]
     answer = []

time: 105 us -> 105 us (level)
  no operation moved by 1% of the time
where the time goes in v7:
time: 105 us
  blocking collectives  65.2 us (62%)
  starting transfers between devices  17 us (16%)
  Pallas kernels  13.7 us (13%)
  waiting for transfers between devices  7.24 us (7%)
  between operations  1.31 us (1%)
    all_to_all x4, blocking collectives, exchange(): return lax.all_to_all(x, axis, 0, 0, tiled=True)  56.7 us
    all_to_all x1, starting transfers between devices, exchange(): return lax.all_to_all(x, axis, 0, 0, tiled=True)  17 us
    all_gather x1, blocking collectives, shards(): pair = lax.all_gather(week_factors, 'core', axis=0, tiled=True)  8.49 us
    all_to_all x1, waiting for transfers between devices, exchange(): return lax.all_to_all(x, axis, 0, 0, tiled=True)  7.24 us
    pallas_call x1, Pallas kernels, prepare(): pl.pallas_call(prepare_kernel, out_shape=(pltpu.VMEM(values.shape, jnp.fl...  4.39 us
    pallas_call x1, Pallas kernels, user_equations(): pl.pallas_call(user_kernel, out_shape=(pltpu.VMEM((UBD * B, WIDTH), LINK)...  2.92 us
    pallas_call x2, Pallas kernels, solve(): pl.pallas_call(solve_kernel, out_shape=(jax.ShapeDtypeStruct((T, R), f32)...  2.87 us
    pallas_call x1, Pallas kernels, item_equations(): pl.pallas_call(item_kernel, out_shape=pltpu.VMEM((IBD * B, WIDTH), LINK),...  2.72 us
  transfers between devices with their start and end apart: 1, of which 1 were waited for; matrix products, arithmetic and copies ran while one was open for 0% of the time, Pallas kernels for 4%

profile of v7, /device:TPU:1, one launch (start us, length us, event | category | flops | bytes accessed | tf_op | source)
XLA Modules:
  0.0 105.1 jit_solution(17223865781734294667)
XLA Ops:
  0.6 8.5 %all-gather = f32[2,4,32]{2,1,0:T(4,128)S(1)} all-gather(f32[1,4,32]{2,1,0:T(4,128)} %bitcast.25), channel_id=1, replica_groups=mesh['z'=8,'core'=2,'x'=4,'y'=8] {'core'}, dimensions={0}, use_global_device_ids=true | all-gather | bytes 1536 | tf_op jit(solution)/shard_map/all_gather | solution.py:406
  9.1 0.8 shard_map.87
  9.9 17.0 %all-to-all-start = ((bf16[256,2,128]{2,1,0:T(2,128)(2,1)}), bf16[256,2,128]{2,1,0:T(2,128)(2,1)S(1)}, u32[]{:S(2)}, u32[]{:S(2)}) async-start(bf16[256,2,128]{2,1,0:T(2,128)(2,1)} %shard_map.87), calls=%async_computation | async-start | bytes 262144 | tf_op jit(solution)/shard_map/all_to_all | solution.py:401
  27.6 4.4 %shard_map.86 = (f8e4m3fn[2,64,4096]{2,1,0:T(32,128)(4,1)S(1)}, f8e4m3fn[2,64,4096]{2,1,0:T(32,128)(4,1)S(1)}, bf16[2,64,4096]{2,1,0:T(8,128)(2,1)S(1)}, f32[32,...) custom-call(s32[2,3]{1,0:T(2,128)} %bitcast.26, s32[1,1]{1,0:T(1,128)S(6)} %copy.12.counts, ...), custom_call_target="tpu_custom_call" | custom-call | tf_op jit(solution)/shard_map/pallas_call | solution.py:313
  32.0 7.2 %all-to-all-done.weeks = bf16[256,2,128]{2,1,0:T(2,128)(2,1)S(1)} async-done(((bf16[256,2,128]{2,1,0:T(2,128)(2,1)}), bf16[256,2,128]{2,1,0:T(2,128)(2,1)S(1)}, u32[]{:S(2)}, u32[]{:S(2)}) %all-to-all-start) | async-done | bytes 131104 | tf_op jit(solution)/shard_map/all_to_all | solution.py:401
  39.2 2.9 %shard_map.88 = (bf16[256,640]{1,0:T(8,128)(2,1)S(1)}, bf16[2,64,640]{2,1,0:T(8,128)(2,1)S(1)}, f32[2,16,64,128]{3,2,1,0:T(8,128)S(1)}) custom-call(s32[2,3]{1,0:T(2,128)S(1)} %get-tuple-element.14.places, bf16[256,2,128]{2,1,0:T(2,128)(2,1)S(1)} %all-to-all-done.weeks, f8e4m3fn[2,64,4096]{2,1,0:T(32,128)(4,1)S(1)} %get-tuple-element.15.mask, ...), custom_call_target="tpu_custom_call" | custom-call | tf_op jit(solution)/shard_map/pallas_call | solution.py:334
  42.1 13.4 %all_to_all.43 = bf16[32,8,640]{2,1,0:T(8,128)(2,1)S(1)} all-to-all(bf16[32,8,640]{2,1,0:T(8,128)(2,1)S(1)} %bitcast.17), channel_id=1, replica_groups=mesh['z'=8,'core'=2,'x'=4,'y'=8] {'x','y'}, dimensions={0} | all-to-all | bytes 655360 | tf_op jit(solution)/shard_map/all_to_all | solution.py:401
  55.5 1.4 %shard_map.89 = (f32[8,32]{1,0:T(8,128)}, bf16[256,128]{1,0:T(8,128)(2,1)S(1)}) custom-call(bf16[256,640]{1,0:T(8,128)(2,1)S(1)} %bitcast.14), custom_call_target="tpu_custom_call" | custom-call | tf_op jit(solution)/shard_map/pallas_call | solution.py:358
  56.9 15.6 %all_to_all.44 = bf16[32,8,128]{2,1,0:T(8,128)(2,1)S(1)} all-to-all(bf16[32,8,128]{2,1,0:T(8,128)(2,1)S(1)} %bitcast.19), channel_id=1, replica_groups=mesh['z'=8,'core'=2,'x'=4,'y'=8] {'x','y'}, dimensions={0} | all-to-all | bytes 131072 | tf_op jit(solution)/shard_map/all_to_all | solution.py:401
  72.5 2.7 %shard_map.90 = bf16[128,640]{1,0:T(8,128)(2,1)S(1)} custom-call(s32[2,3]{1,0:T(2,128)S(1)} %get-tuple-element.14.places, f8e4m3fn[2,64,4096]{2,1,0:T(32,128)(4,1)S(1)} %get-tuple-element.21.turned, f32[2,16,64,128]{3,2,1,0:T(8,128)S(1)} %get-tuple-element.22.moment, bf16[256,128]{1,0:T(8,128)(2,1)S(1)} %bitcast.18, ...), custom_call_target="tpu_custom_call" | custom-call | tf_op jit(solution)/shard_map/pallas_call | solution.py:348
  75.3 17.3 %all_to_all.45 = bf16[16,8,640]{2,1,0:T(8,128)(2,1)S(1)} all-to-all(bf16[16,8,640]{2,1,0:T(8,128)(2,1)S(1)} %bitcast.15), channel_id=1, replica_groups=mesh['z'=8,'core'=2,'x'=4,'y'=8] {'z','core'}, dimensions={0} | all-to-all | bytes 327680 | tf_op jit(solution)/shard_map/all_to_all | solution.py:401
  92.5 1.4 %shard_map.91 = (f32[8,32]{1,0:T(8,128)}, f32[16,8,128]{2,1,0:T(8,128)S(1)}) custom-call(bf16[128,640]{1,0:T(8,128)(2,1)S(1)} %bitcast.16), custom_call_target="tpu_custom_call" | custom-call | tf_op jit(solution)/shard_map/pallas_call | solution.py:358
  94.0 10.4 %all_to_all.46 = f32[16,8,128]{2,1,0:T(8,128)S(1)} all-to-all(f32[16,8,128]{2,1,0:T(8,128)S(1)} %get-tuple-element.25), channel_id=1, replica_groups=mesh['z'=8,'core'=2,'x'=4,'y'=8] {'z','core'}, dimensions={0} | all-to-all | bytes 131072 | tf_op jit(solution)/shard_map/all_to_all | solution.py:401
  104.4 0.7 copy.11
Async XLA Ops:
  9.9 29.3 %all-to-all-start = ((bf16[256,2,128]{2,1,0:T(2,128)(2,1)}), bf16[256,2,128]{2,1,0:T(2,128)(2,1)S(1)}, u32[]{:S(2)}, u32[]{:S(2)}) async-start(bf16[256,2,128]{2,1,0:T(2,128)(2,1)} %shard_map.87), calls=%async_computation | async-start | bytes 262144 | tf_op jit(solution)/shard_map/all_to_all | solution.py:401
